TPU v7x, 32 devices: a whole 2x2x4 slice. The times are simulated.
32 devices in a mesh: ta: 8 (over y, x, core), sa: 4 (over z).
Axes of the slice: x: 2, y: 2, z: 4, core: 2. Of those that a mesh axis runs over, the one named last changes fastest.
Arguments:
- null_vectors: bfloat16 [2, 24, 4, 3, 32, 16, 128], P(None, None, None, None, 'ta', 'sa'), may hold values from -0.15234375 to 0.15234375
- gauge_links: bfloat16 [2, 4, 3, 3, 32, 16, 128], P(None, None, None, None, 'ta', 'sa'), may hold values from -3.59375 to 3.59375
- coarse_in: float32 [8, 4, 8, 96], P('ta', 'sa'), may hold values from -6 to 6
Outputs:
- coarse_links: float32 [8, 4, 8, 5, 4608], P('ta', 'sa')
- coarse_out: float32 [8, 4, 8, 96], P('ta', 'sa')
All inputs are finite; a program needn't handle non-finite values.
Results may differ from a plain program's by a relative error of at most 0.0018.
Values may be sent and summed in bfloat16 or wider, within the bound.
A program may use at most 256 MiB of HBM per device.

v0:
```python
import jax
import jax.numpy as jnp
from jax import lax
from jax.sharding import PartitionSpec as P

LAT_Y = 4
LAT_X = 32


gamma_rows = (
    ((2, 1.0, 0.0), (3, 1.0, 0.0), (0, 1.0, 0.0), (1, 1.0, 0.0)),
    ((2, 0.0, -1.0), (3, 0.0, 1.0), (0, 0.0, 1.0), (1, 0.0, -1.0)),
    ((3, -1.0, 0.0), (2, 1.0, 0.0), (1, 1.0, 0.0), (0, -1.0, 0.0)),
    ((3, 0.0, -1.0), (2, 0.0, -1.0), (1, 0.0, 1.0), (0, 0.0, 1.0)),
)
diag_shift = 1.0


def shifted_2(value, axis, steps):
    count = lax.axis_size(axis)
    pairs = [(source, (source + steps) % count) for source in range(count)]
    return lax.ppermute(value, axis, pairs)


def site_order(plane_size, width, depth):
    agg_cols = width // 4
    positions = jnp.arange(depth * plane_size, dtype=jnp.int32)
    local_count = depth * 16
    local = positions % local_count
    aggregate = positions // local_count
    agg_row = aggregate // agg_cols
    agg_col = aggregate % agg_cols
    outer_coord = local // 16
    row_inside = local // 4 % 4
    col_inside = local % 4
    return outer_coord * plane_size + (agg_row * 4 + row_inside) * width + agg_col * 4 + col_inside


def regroup(field, order, depth):
    leading = field.shape[:-3]
    plane_size = field.shape[-1]
    flat = field.reshape(leading + (depth * plane_size,))
    picked = jnp.take(flat, order, axis=-1)
    picked = picked.reshape(leading + (-1, depth * 16))
    return jnp.moveaxis(picked, -2, 0)


def color_agg(links, vectors):
    real_part = 0.0
    imag_part = 0.0
    for colour in range(3):
        link_r = links[:, 0, :, colour][:, None, None].astype(jnp.float32)
        link_i = links[:, 1, :, colour][:, None, None].astype(jnp.float32)
        vector_r = vectors[:, 0, :, :, colour][:, :, :, None].astype(jnp.float32)
        vector_i = vectors[:, 1, :, :, colour][:, :, :, None].astype(jnp.float32)
        real_part = real_part + link_r * vector_r - link_i * vector_i
        imag_part = imag_part + link_r * vector_i + link_i * vector_r
    return (real_part, imag_part)


def hop_agg(real_part, imag_part, direction):
    same_hop = jnp.stack([-0.5 * real_part, -0.5 * imag_part], axis=1).astype(jnp.bfloat16)
    rows_real = []
    rows_imag = []
    for spin in range(4):
        source, phase_r, phase_i = gamma_rows[direction][spin]
        rows_real.append(phase_r * real_part[:, :, source] - phase_i * imag_part[:, :, source])
        rows_imag.append(phase_r * imag_part[:, :, source] + phase_i * real_part[:, :, source])
    cross_hop = (
        0.5 * jnp.stack([jnp.stack(rows_real, 2), jnp.stack(rows_imag, 2)], axis=1)
    ).astype(jnp.bfloat16)
    return (same_hop, cross_hop)


def pair_product(left_side, right_side):
    return jnp.einsum(
        "arvsck,aqwsck->arvqw", left_side, right_side, preferred_element_type=jnp.float32
    )


def contract_agg(vectors, same_hop, cross_hop):
    vector_count = vectors.shape[2]
    hops = jnp.concatenate([same_hop, cross_hop], axis=2)
    row_blocks = []
    for chirality in range(2):
        spin_range = slice(2 * chirality, 2 * chirality + 2)
        product = pair_product(vectors[:, :, :, spin_range], hops[:, :, :, spin_range])
        real_part = product[..., 0, :, 0, :] + product[..., 1, :, 1, :]
        imag_part = product[..., 0, :, 1, :] - product[..., 1, :, 0, :]
        components = []
        for component in (real_part, imag_part):
            same_cols = component[..., :vector_count]
            cross_cols = component[..., vector_count:]
            if chirality == 0:
                components.append(jnp.concatenate([same_cols, cross_cols], axis=-1))
            else:
                components.append(jnp.concatenate([cross_cols, same_cols], axis=-1))
        row_blocks.append(jnp.stack(components, axis=-3))
    return jnp.concatenate(row_blocks, axis=-2)


def gram_agg(vectors):
    row_blocks = []
    for chirality in range(2):
        spin_range = slice(2 * chirality, 2 * chirality + 2)
        product = pair_product(vectors[:, :, :, spin_range], vectors[:, :, :, spin_range])
        real_part = product[..., 0, :, 0, :] + product[..., 1, :, 1, :]
        imag_part = product[..., 0, :, 1, :] - product[..., 1, :, 0, :]
        components = []
        for component in (real_part, imag_part):
            zero_block = jnp.zeros_like(component)
            if chirality == 0:
                components.append(jnp.concatenate([component, zero_block], axis=-1))
            else:
                components.append(jnp.concatenate([zero_block, component], axis=-1))
        row_blocks.append(jnp.stack(components, axis=-3))
    return jnp.concatenate(row_blocks, axis=-2)


def adjoint(blocks):
    vector_count = blocks.shape[-1] // 2
    chirality_sign = jnp.concatenate(
        [jnp.ones(vector_count, jnp.float32), -jnp.ones(vector_count, jnp.float32)]
    )
    outer_sign = chirality_sign[:, None] * chirality_sign[None, :]
    real_part = outer_sign * jnp.swapaxes(blocks[..., 0, :, :], -1, -2)
    imag_part = -outer_sign * jnp.swapaxes(blocks[..., 1, :, :], -1, -2)
    return jnp.stack([real_part, imag_part], axis=-3)


def direction_blocks(vec_agg, shifted_agg, link_agg, direction, weights):
    real_part, imag_part = color_agg(link_agg, shifted_agg)
    same_hop, cross_hop = hop_agg(real_part, imag_part, direction)
    results = []
    for weight in weights:
        operand = vec_agg * weight
        results.append(contract_agg(operand, same_hop, cross_hop))
    return results


def grid(blocks):
    return blocks.reshape((1, 1, LAT_Y // 4, LAT_X // 4) + blocks.shape[1:])


def matvec(blocks, coarse_vector):

    def times_vector(matrix, column):
        return jnp.einsum("...ij,...j->...i", matrix, column, precision=lax.Precision.HIGHEST)

    real_part = times_vector(blocks[..., 0, :, :], coarse_vector[..., 0, :]) - times_vector(
        blocks[..., 1, :, :], coarse_vector[..., 1, :]
    )
    imag_part = times_vector(blocks[..., 0, :, :], coarse_vector[..., 1, :]) + times_vector(
        blocks[..., 1, :, :], coarse_vector[..., 0, :]
    )
    return jnp.stack([real_part, imag_part], axis=-2)


def per_device(null_vectors, gauge_links, coarse_in):
    plane_size = null_vectors.shape[-1]
    full_order = site_order(plane_size, LAT_X, 16)
    vec_agg = regroup(null_vectors, full_order, 16)
    local = jnp.arange(256, dtype=jnp.int32)
    coords = (local // 64, local // 16 % 4, local // 4 % 4, local % 4)
    plane_index = jnp.arange(plane_size, dtype=jnp.int32)
    next_col = plane_index // LAT_X * LAT_X + (plane_index % LAT_X + 1) % LAT_X
    diagonal = diag_shift * gram_agg(vec_agg)
    first_t = lax.slice_in_dim(null_vectors, 0, 1, axis=4)
    first_z = lax.slice_in_dim(null_vectors, 0, 1, axis=5)
    face_t = shifted_2(first_t, "ta", -1)
    face_z = shifted_2(first_z, "sa", -1)
    ahead_t = jnp.concatenate([lax.slice_in_dim(null_vectors, 1, 4, axis=4), face_t], axis=4)
    ahead_z = jnp.concatenate([lax.slice_in_dim(null_vectors, 1, 4, axis=5), face_z], axis=5)
    link_t = None
    link_z = None
    forward = []
    for direction in range(4):
        if direction == 0:
            shifted = ahead_t
        elif direction == 1:
            shifted = ahead_z
        elif direction == 2:
            shifted = jnp.roll(null_vectors, -LAT_X, axis=-1)
        else:
            shifted = jnp.take(null_vectors, next_col, axis=-1)
        shifted_agg = regroup(shifted, full_order, 16)
        link_agg = regroup(gauge_links[:, direction], full_order, 16)
        boundary = coords[direction] == 3
        inner_weight = jnp.where(boundary, 0.0, 1.0).astype(jnp.bfloat16)
        outer_weight = jnp.where(boundary, 1.0, 0.0).astype(jnp.bfloat16)
        weights = (inner_weight, outer_weight)
        parts = direction_blocks(vec_agg, shifted_agg, link_agg, direction, weights)
        diagonal = diagonal + parts[0] + adjoint(parts[0])
        forward.append(grid(parts[1]))
    link_t = forward[0]
    link_z = forward[1]
    link_y = forward[2]
    link_x = forward[3]
    diagonal = grid(diagonal)
    coarse_blocks = jnp.stack([diagonal, link_t, link_z, link_y, link_x], axis=-4)
    reverse_y = adjoint(link_y)
    reverse_x = adjoint(link_x)
    reverse_t = adjoint(link_t)
    reverse_z = adjoint(link_z)
    coarse_vector = coarse_in.reshape(1, 1, LAT_Y // 4, LAT_X // 4, 2, -1)
    for step_number in range(2):
        result = matvec(diagonal, coarse_vector)
        ahead_coarse_t = shifted_2(coarse_vector, "ta", -1)
        result = result + matvec(link_t, ahead_coarse_t)
        result = result + shifted_2(matvec(reverse_t, coarse_vector), "ta", 1)
        ahead_coarse_z = shifted_2(coarse_vector, "sa", -1)
        result = result + matvec(link_z, ahead_coarse_z)
        result = result + shifted_2(matvec(reverse_z, coarse_vector), "sa", 1)
        result = result + matvec(link_y, jnp.roll(coarse_vector, -1, axis=2))
        result = result + jnp.roll(matvec(reverse_y, coarse_vector), 1, axis=2)
        result = result + matvec(link_x, jnp.roll(coarse_vector, -1, axis=3))
        result = result + jnp.roll(matvec(reverse_x, coarse_vector), 1, axis=3)
        coarse_vector = result
    block_size = coarse_blocks.shape[-3] * coarse_blocks.shape[-2] * coarse_blocks.shape[-1]
    return (
        coarse_blocks.reshape(1, 1, -1, 5, block_size),
        coarse_vector.reshape(1, 1, -1, coarse_in.shape[-1]),
    )


def solution(mesh):
    placed = (
        P(None, None, None, None, "ta", "sa", None),
        P(None, None, None, None, "ta", "sa", None),
        P("ta", "sa", None, None),
    )
    return jax.shard_map(
        per_device,
        mesh=mesh,
        in_specs=placed,
        out_specs=(P("ta", "sa", None, None, None), P("ta", "sa", None, None)),
        check_vma=False,
    )
```

profile of v0, /device:TPU:0, one launch (start us, length us, event | category | flops | bytes accessed | tf_op | source)
XLA Modules:
  0.0 834.0 jit_solution(15702232137116805377)
XLA Ops:
  19.8 15.9 %copy.474 = bf16[2,24,4,3,4,4,128]{1,4,3,2,5,0,6:T(4,128)(2,1)} copy(bf16[2,24,4,3,4,4,128]{6,5,4,3,2,1,0:T(4,128)(2,1)S(1)} %copy-done) | data formatting | bytes 4718592 | tf_op args[0]
  48.4 22.2 %gather_fusion.8 = bf16[2048,2,3,3]{3,1,2,0:T(2,128)(2,1)} fusion(bf16[2,3,3,2048]{2,0,3,1:T(2,128)(2,1)} %bitcast.1394, s32[2048]{0:T(1024)S(1)} %broadcast_clamp_fusion), kind=kCustom, calls=%fused_computation.8.clone | custom fusion | bytes 155648 | tf_op jit(solution)/shard_map/jit(_take)/gather | solution.py:43
  70.6 22.3 %gather_fusion.4 = bf16[2048,2,3,3]{3,1,2,0:T(2,128)(2,1)} fusion(bf16[2,3,3,2048]{2,0,3,1:T(2,128)(2,1)} %bitcast.1395, s32[2048]{0:T(1024)S(1)} %broadcast_clamp_fusion), kind=kCustom, calls=%fused_computation.6.clone | custom fusion | bytes 155648 | tf_op jit(solution)/shard_map/jit(_take)/gather | solution.py:43
  98.6 22.2 %gather_fusion.2 = bf16[2048,2,3,3]{3,1,2,0:T(2,128)(2,1)} fusion(bf16[2,3,3,2048]{2,0,3,1:T(2,128)(2,1)} %bitcast.1396, s32[2048]{0:T(1024)S(1)} %broadcast_clamp_fusion), kind=kCustom, calls=%fused_computation.1.clone | custom fusion | bytes 155648 | tf_op jit(solution)/shard_map/jit(_take)/gather | solution.py:43
  126.5 22.3 %gather_fusion.6 = bf16[2048,2,3,3]{3,1,2,0:T(2,128)(2,1)} fusion(bf16[2,3,3,2048]{2,0,3,1:T(2,128)(2,1)} %bitcast.1397, s32[2048]{0:T(1024)S(1)} %broadcast_clamp_fusion), kind=kCustom, calls=%fused_computation.7.clone | custom fusion | bytes 155648 | tf_op jit(solution)/shard_map/jit(_take)/gather | solution.py:43
  148.8 18.3 %broadcast_select_fusion.6 = (bf16[2048,2,3,3]{3,1,2,0:T(2,128)(2,1)}, bf16[2048,2,3,3]{3,1,2,0:T(2,128)(2,1)}, bf16[2048,2,3,3]{3,1,2,0:T(2,128)(2,1)}, bf16[2048,2,3,3]{3,1,2,0:T(2,128)(2,1)}) fusion(bf16[2048,2,3,3]{3,1,2,0:T(2,128)(2,1)} %gather_fusion.8, pred[2048]{0:T(1024)(128)(4,1)S(1)} %compare_and_fusion, bf16[2048,2,3,3]{3,1,2,0:T(2,128)(2,1)} %gather_fusion.4, ...), kind=kLoop, calls=%fused_computation.16 | loop fusion | flops 147456 | bytes 591872 | tf_op jit(solution)/shard_map/jit(_take)/select_n | solution.py:43
  187.2 19.2 %gather_fusion = bf16[128,2,24,4,3,4,4]{2,5,4,3,6,1,0:T(4,128)(2,1)} fusion(bf16[2,24,4,3,4,4,128]{1,4,3,2,5,0,6:T(4,128)(2,1)} %copy.474, s32[1024]{0:T(1024)S(1)} %pad_clamp_fusion), kind=kCustom, calls=%fused_computation.9 | custom fusion | bytes 4719104 | tf_op jit(solution)/shard_map/jit(_take)/gather | solution.py:185
  206.4 10.1 %copy.750 = bf16[2,24,4,3,4,4,128]{1,2,6,5,4,3,0:T(4,128)(2,1)S(1)} copy(bf16[2,24,4,3,4,4,128]{1,4,3,2,5,0,6:T(4,128)(2,1)} %bitcast.1383) | data formatting | bytes 4718592 | tf_op jit(solution)/shard_map/jit(_take)/gather | solution.py:185
  221.4 11.2 %broadcast_select_fusion.5 = bf16[2,24,4,3,2048]{1,2,4,3,0:T(4,128)(2,1)} fusion(bf16[2,24,4,3,2048]{1,2,4,3,0:T(4,128)(2,1)S(1)} %bitcast.1378, pred[2048]{0:T(1024)(128)(4,1)S(1)} %bitcast.1528), kind=kLoop, calls=%fused_computation.15 | loop fusion | flops 1179648 | bytes 4720640 | tf_op jit(solution)/shard_map/jit(_take)/select_n | solution.py:185
  239.9 13.9 %copy.790 = bf16[2,24,4,3,4,4,128]{1,2,6,5,4,3,0:T(4,128)(2,1)} copy(bf16[2,24,4,3,4,4,128]{6,5,4,3,2,1,0:T(4,128)(2,1)S(1)} %copy-done) | data formatting | bytes 4718592 | tf_op jit(solution)/shard_map/reshape | solution.py:42
  267.2 19.2 %copy.796 = bf16[2,24,4,3,4,4,128]{1,2,6,5,4,3,0:T(4,128)(2,1)} copy(bf16[2,24,4,3,4,4,128]{6,5,4,3,2,1,0:T(4,128)(2,1)} %pad_maximum_fusion.8) | data formatting | bytes 4718592 | tf_op jit(solution)/shard_map/reshape | solution.py:42
  286.4 34.8 %gather_fusion.7 = bf16[2048,2,24,4,3]{2,3,4,1,0:T(4,128)(2,1)} fusion(bf16[2,24,4,3,2048]{1,2,4,3,0:T(4,128)(2,1)} %bitcast.1381, s32[2048]{0:T(1024)S(1)} %broadcast_clamp_fusion), kind=kCustom, calls=%fused_computation.4.clone | custom fusion | bytes 4726784 | tf_op jit(solution)/shard_map/jit(_take)/gather | solution.py:43
  321.2 34.7 %gather_fusion.1 = bf16[2048,2,24,4,3]{2,3,4,1,0:T(4,128)(2,1)} fusion(bf16[2,24,4,3,2048]{1,2,4,3,0:T(4,128)(2,1)} %bitcast.1379, s32[2048]{0:T(1024)S(1)} %broadcast_clamp_fusion), kind=kCustom, calls=%fused_computation.clone | custom fusion | bytes 4726784 | tf_op jit(solution)/shard_map/jit(_take)/gather | solution.py:43
  355.9 35.2 %gather_fusion.9 = bf16[2048,2,24,4,3]{2,3,4,1,0:T(4,128)(2,1)} fusion(bf16[2,24,4,3,2048]{1,2,4,3,0:T(4,128)(2,1)} %broadcast_select_fusion.5, s32[2048]{0:T(1024)S(1)} %broadcast_clamp_fusion), kind=kCustom, calls=%fused_computation.5.clone | custom fusion | bytes 4726784 | tf_op jit(solution)/shard_map/jit(_take)/gather | solution.py:43
  398.9 13.9 %copy.794 = bf16[2,24,4,3,4,4,128]{1,2,6,5,4,3,0:T(4,128)(2,1)} copy(bf16[2,24,4,3,4,4,128]{6,5,4,3,2,1,0:T(4,128)(2,1)S(1)} %pad_maximum_fusion.7) | data formatting | bytes 4718592 | tf_op jit(solution)/shard_map/reshape | solution.py:42
  412.7 34.8 %gather_fusion.5 = bf16[2048,2,24,4,3]{2,3,4,1,0:T(4,128)(2,1)} fusion(bf16[2,24,4,3,2048]{1,2,4,3,0:T(4,128)(2,1)} %bitcast.1382, s32[2048]{0:T(1024)S(1)} %broadcast_clamp_fusion), kind=kCustom, calls=%fused_computation.3.clone | custom fusion | bytes 4726784 | tf_op jit(solution)/shard_map/jit(_take)/gather | solution.py:43
  450.7 13.9 %copy.792 = bf16[2,24,4,3,4,4,128]{1,2,6,5,4,3,0:T(4,128)(2,1)} copy(bf16[2,24,4,3,4,4,128]{6,5,4,3,2,1,0:T(4,128)(2,1)S(1)} %pad_maximum_fusion.6) | data formatting | bytes 4718592 | tf_op jit(solution)/shard_map/reshape | solution.py:42
  464.5 34.8 %gather_fusion.3 = bf16[2048,2,24,4,3]{2,3,4,1,0:T(4,128)(2,1)} fusion(bf16[2,24,4,3,2048]{1,2,4,3,0:T(4,128)(2,1)} %bitcast.1380, s32[2048]{0:T(1024)S(1)} %broadcast_clamp_fusion), kind=kCustom, calls=%fused_computation.2.clone | custom fusion | bytes 4726784 | tf_op jit(solution)/shard_map/jit(_take)/gather | solution.py:43
  499.4 45.6 %broadcast_select_fusion = (bf16[2048,2,24,4,3]{2,3,4,1,0:T(4,128)(2,1)}, bf16[2048,2,24,4,3]{2,3,4,1,0:T(4,128)(2,1)}, bf16[2048,2,24,4,3]{2,3,4,1,0:T(4,128)(2...) fusion(bf16[2048,2,24,4,3]{2,3,4,1,0:T(4,128)(2,1)} %gather_fusion.9, ...), kind=kLoop, calls=%fused_computation.10 | loop fusion | flops 5898240 | bytes 23595008 | tf_op jit(solution)/shard_map/jit(_take)/select_n | solution.py:43
  544.9 16.6 %copy.330 = bf16[2,24,4,3,8,256]{5,1,2,3,0,4:T(8,128)(2,1)S(1)} copy(bf16[2,24,4,3,8,256]{1,2,3,0,5,4:T(4,128)(2,1)} %bitcast.1377) | data formatting | bytes 4718592 | tf_op jit(solution)/shard_map/reshape | solution.py:44
  566.1 12.6 %copy.751 = bf16[2,24,4,3,8,256]{5,4,1,3,2,0:T(8,128)(2,1)S(1)} copy(bf16[2,24,4,3,8,256]{1,2,3,0,5,4:T(4,128)(2,1)} %bitcast.1376) | data formatting | bytes 4718592 | tf_op jit(solution)/shard_map/reshape | solution.py:44
  587.3 12.6 %copy.708 = bf16[2,24,4,3,8,256]{5,4,1,3,2,0:T(8,128)(2,1)S(1)} copy(bf16[2,24,4,3,8,256]{1,2,3,0,5,4:T(4,128)(2,1)} %bitcast.1375) | data formatting | bytes 4718592 | tf_op jit(solution)/shard_map/reshape | solution.py:44
  608.5 13.1 %copy.722 = bf16[2,24,4,3,8,256]{5,4,1,3,2,0:T(8,128)(2,1)S(1)} copy(bf16[2,24,4,3,8,256]{1,2,3,0,5,4:T(4,128)(2,1)} %bitcast.1374) | data formatting | bytes 4718592 | tf_op jit(solution)/shard_map/reshape | solution.py:44
  629.9 12.6 %copy.738 = bf16[2,24,4,3,8,256]{5,4,1,3,2,0:T(8,128)(2,1)S(1)} copy(bf16[2,24,4,3,8,256]{1,2,3,0,5,4:T(4,128)(2,1)} %bitcast.1373) | data formatting | bytes 4718592 | tf_op jit(solution)/shard_map/reshape | solution.py:44
  (590 shorter events, 318.6 us)
Async XLA Ops:
  2.0 804.1 %collective-permute-start.4 = (f32[1,1,1,8,2,48]{5,4,3,2,1,0:T(2,128)}, f32[1,1,1,8,2,48]{5,4,3,2,1,0:T(2,128)}, u32[]{:S(2)}, u32[]{:S(2)}) collective-permute-start(f32[1,1,1,8,2,48]{5,4,3,2,1,0:T(2,128)} %reshape.2347), channel_id=1, source_target_pairs={{0,3},{1,0},{2,1},{3,2},{4,7},{5,4},{6,5},{7,6},{8,11},{9,8},{10,9... | collective-permute-start | bytes 9224 | tf_op jit(solution)/shard_map/ppermute | solution.py:22
  7.0 791.5 %collective-permute-start.2 = (f32[1,1,1,8,2,48]{5,4,3,2,1,0:T(2,128)}, f32[1,1,1,8,2,48]{5,4,3,2,1,0:T(2,128)}, u32[]{:S(2)}, u32[]{:S(2)}) collective-permute-start(f32[1,1,1,8,2,48]{5,4,3,2,1,0:T(2,128)} %reshape.2347), channel_id=1, source_target_pairs={{0,28},{4,0},{8,4},{12,8},{16,12},{20,16},{24,20},{28,24},{1,29},{... | collective-permute-start | bytes 9224 | tf_op jit(solution)/shard_map/ppermute | solution.py:22
  10.7 436.9 %collective-permute-start = (bf16[2,24,4,3,1,4,128]{6,5,4,3,2,1,0:T(4,128)(2,1)}, bf16[2,24,4,3,1,4,128]{6,5,4,3,2,1,0:T(4,128)(2,1)S(1)}, u32[]{:S(2)}, u32[]{:S(2)}) collective-permute-start(bf16[2,24,4,3,1,4,128]{6,5,4,3,2,1,0:T(4,128)(2,1)} %slice.990), channel_id=1, source_target_pairs={{0,28},{4,0},{8,4},{12,8},{16,12},{20,16},{24,20},{28,24},{1,29},{... | collective-permute-start | bytes 1769480 | tf_op jit(solution)/shard_map/ppermute | solution.py:22
  15.4 377.3 %collective-permute-start.1 = (bf16[2,24,4,3,4,1,128]{6,1,5,4,3,2,0:T(8,128)(2,1)}, bf16[2,24,4,3,4,1,128]{6,1,5,4,3,2,0:T(8,128)(2,1)}, u32[]{:S(2)}, u32[]{:S(2)}) collective-permute-start(bf16[2,24,4,3,4,1,128]{6,1,5,4,3,2,0:T(8,128)(2,1)} %copy.801), channel_id=1, source_target_pairs={{0,3},{1,0},{2,1},{3,2},{4,7},{5,4},{6,5},{7,6},{8,11},{9,8},{10,9... | collective-permute-start | bytes 1769480 | tf_op jit(solution)/shard_map/ppermute | solution.py:22
  19.8 15.9 %copy-start.89 = (f32[48]{0:T(128)S(1)}, f32[48]{0:T(128)}, u32[]{:S(2)}) copy-start(f32[48]{0:T(128)} %constant.240.clone.1) | copy-start | bytes 580
  35.8 218.0 %copy-start.10 = (f32[48,48]{0,1:T(8,128)}, f32[48,48]{0,1:T(8,128)S(1)}, u32[]{:S(2)}) copy-start(f32[48,48]{0,1:T(8,128)S(1)} %get-tuple-element.275) | copy-start | bytes 27652
  35.8 218.7 %copy-start.12 = (f32[48,48]{0,1:T(8,128)}, f32[48,48]{0,1:T(8,128)S(1)}, u32[]{:S(2)}) copy-start(f32[48,48]{0,1:T(8,128)S(1)} %get-tuple-element.276) | copy-start | bytes 27652
  206.4 10.1 %copy-start.1 = (bf16[2,24,4,3,4,4,96]{6,5,4,3,2,1,0:T(4,128)(2,1)S(1)}, bf16[2,24,4,3,4,4,96]{6,5,4,3,2,1,0:T(4,128)(2,1)}, u32[]{:S(2)}) copy-start(bf16[2,24,4,3,4,4,96]{6,5,4,3,2,1,0:T(4,128)(2,1)} %slice.1071) | copy-start | bytes 5308420
  239.8 15.3 %copy-start.67 = (f32[8,3,256]{2,0,1:T(8,128)S(1)}, f32[8,3,256]{2,0,1:T(8,128)}, u32[]{:S(2)}) copy-start(f32[8,3,256]{2,0,1:T(8,128)} %get-tuple-element.240) | copy-start | bytes 73732
  239.8 15.3 %copy-start.66 = (f32[8,3,256]{2,0,1:T(8,128)S(1)}, f32[8,3,256]{2,0,1:T(8,128)}, u32[]{:S(2)}) copy-start(f32[8,3,256]{2,0,1:T(8,128)} %get-tuple-element.241) | copy-start | bytes 73732
  239.9 15.3 %copy-start.65 = (f32[8,3,256]{2,0,1:T(8,128)S(1)}, f32[8,3,256]{2,0,1:T(8,128)}, u32[]{:S(2)}) copy-start(f32[8,3,256]{2,0,1:T(8,128)} %get-tuple-element.242) | copy-start | bytes 73732
  239.9 15.4 %copy-start.64 = (f32[8,3,256]{2,0,1:T(8,128)S(1)}, f32[8,3,256]{2,0,1:T(8,128)}, u32[]{:S(2)}) copy-start(f32[8,3,256]{2,0,1:T(8,128)} %get-tuple-element.243) | copy-start | bytes 73732
  239.9 15.4 %copy-start.63 = (f32[8,3,256]{2,0,1:T(8,128)S(1)}, f32[8,3,256]{2,0,1:T(8,128)}, u32[]{:S(2)}) copy-start(f32[8,3,256]{2,0,1:T(8,128)} %get-tuple-element.244) | copy-start | bytes 73732
  668.3 13.4 %copy-start.7 = (f32[8,24,4,3,256]{4,1,2,3,0:T(8,128)S(1)}, f32[8,24,4,3,256]{4,1,2,3,0:T(8,128)}, u32[]{:S(2)}) copy-start(f32[8,24,4,3,256]{4,1,2,3,0:T(8,128)} %get-tuple-element.7) | copy-start | bytes 7077892
  669.8 11.9 %copy-start.6 = (f32[8,24,4,3,256]{4,1,2,3,0:T(8,128)S(1)}, f32[8,24,4,3,256]{4,1,2,3,0:T(8,128)}, u32[]{:S(2)}) copy-start(f32[8,24,4,3,256]{4,1,2,3,0:T(8,128)} %get-tuple-element.6) | copy-start | bytes 7077892
  689.0 11.6 %copy-start.15 = (bf16[8,2,24,4,3,256]{5,2,3,4,1,0:T(8,128)(2,1)S(1)}, bf16[8,2,24,4,3,256]{5,2,3,4,1,0:T(8,128)(2,1)}, u32[]{:S(2)}) copy-start(bf16[8,2,24,4,3,256]{5,2,3,4,1,0:T(8,128)(2,1)} %copy-done.14) | copy-start | bytes 7077892
  702.3 9.1 %copy-start.5 = (f32[8,24,4,3,256]{4,1,2,3,0:T(8,128)S(1)}, f32[8,24,4,3,256]{4,1,2,3,0:T(8,128)}, u32[]{:S(2)}) copy-start(f32[8,24,4,3,256]{4,1,2,3,0:T(8,128)} %get-tuple-element.15) | copy-start | bytes 7077892
  783.5 29.8 %collective-permute-start.3 = (f32[1,1,1,8,2,48]{5,3,4,2,1,0:T(8,128)S(1)}, f32[1,1,1,8,2,48]{5,3,4,2,1,0:T(8,128)S(1)}, u32[]{:S(2)}, u32[]{:S(2)}) collective-permute-start(f32[1,1,1,8,2,48]{5,3,4,2,1,0:T(8,128)S(1)} %pad_maximum_fusion.27), channel_id=1, source_target_pairs={{0,4},{4,8},{8,12},{12,16},{16,20},{20,24},{24,28},{28,0},{1,5},{5... | collective-permute-start | bytes 9224 | tf_op jit(solution)/shard_map/ppermute | solution.py:22
  783.6 29.7 %collective-permute-start.5 = (f32[1,1,1,8,2,48]{5,3,4,2,1,0:T(8,128)S(1)}, f32[1,1,1,8,2,48]{5,3,4,2,1,0:T(8,128)S(1)}, u32[]{:S(2)}, u32[]{:S(2)}) collective-permute-start(f32[1,1,1,8,2,48]{5,3,4,2,1,0:T(8,128)S(1)} %pad_maximum_fusion.28), channel_id=1, source_target_pairs={{0,1},{1,2},{2,3},{3,0},{4,5},{5,6},{6,7},{7,4},{8,9},{9,10},{10,1... | collective-permute-start | bytes 9224 | tf_op jit(solution)/shard_map/ppermute | solution.py:22
  795.1 7.9 copy-start.31
  823.2 4.7 collective-permute-start.8
  825.5 4.1 collective-permute-start.6
  827.6 5.5 collective-permute-start.9
  827.7 5.4 collective-permute-start.7
  (81 other events, 277.7 us)
where the time goes:
time: 849 us; the launch traced here: 834 us
  local copies, waits for them, and re-layouts  562 us (66%)
  other arithmetic  165 us (19%)
  matrix products  87.2 us (10%)
  starting transfers between devices  14.2 us (2%)
    gather x9, local copies, waits for them, and re-layouts, regroup(): picked = jnp.take(flat, order, axis=-1)  263 us
    reshape x9, local copies, waits for them, and re-layouts, regroup(): picked = picked.reshape(leading + (-1, depth * 16))  86.3 us
    select_n x2, other arithmetic, regroup(): picked = jnp.take(flat, order, axis=-1)  63.9 us
    reshape x4, local copies, waits for them, and re-layouts, regroup(): flat = field.reshape(leading + (depth * plane_size,))  60.8 us
    dot_general x72, matrix products, times_vector(): jnp.einsum('...ij,...j->...i', matrix, column, precision=lax.Precision.HI...  60.6 us
    gather x2, local copies, waits for them, and re-layouts, per_device(): shifted = jnp.take(null_vectors, next_col, axis=-1)  29.3 us
    unnamed x197, local copies, waits for them, and re-layouts  28 us
    dot_general x18, matrix products, pair_product(): jnp.einsum('arvsck,aqwsck->arvqw', left_side, right_side, preferred_eleme...  26.6 us
  transfers between devices with their start and end apart: 10, of which 1 were waited for; matrix products, arithmetic and copies ran while one was open for 95% of the time, Pallas kernels for 0%

commit v1 on v0

v1 whole, which is shorter than its diff:
```python
import functools

import jax
import jax.numpy as jnp
from jax import lax
from jax.experimental import pallas as pl
from jax.experimental.pallas import tpu as pltpu
from jax.sharding import PartitionSpec as P

LAT_X = 32
MESH = pl.DeviceIdType.MESH

SOURCE = ((2, 3, 0, 1), (2, 3, 0, 1), (3, 2, 1, 0), (3, 2, 1, 0))
ODD_SIGN = (False, True, True, False)
PHASE = ((0, 0), (3, 1), (2, 0), (3, 1))


def turn(re, im, power):
    if power == 0:
        return re, im
    if power == 1:
        return -im, re
    if power == 2:
        return -re, -im
    return im, -re


def hop_rows(same, cross, chi):
    first, second = (same, cross) if chi == 0 else (cross, same)
    of_real = jnp.concatenate([first[0], second[0], first[1], second[1]], 0)
    of_imag = jnp.concatenate([first[1], second[1], -first[0], -second[0]], 0)
    return of_real.astype(jnp.bfloat16), of_imag.astype(jnp.bfloat16)


def place_hops(direction, slot, shifted, u_ref, tz, right):
    links = []
    for q in range(2):
        links.append([[u_ref[tz, pl.ds(((q * 4 + direction) * 3 + row) * 3 + col, 1), :]
                       for col in range(3)] for row in range(3)])
    for c in range(3):
        hops = []
        for s in range(4):
            re = None
            im = None
            for d in range(3):
                lr, li = links[0][c][d], links[1][c][d]
                vr, vi = shifted[s][d]
                term_r = lr * vr - li * vi
                term_i = lr * vi + li * vr
                re = term_r if re is None else re + term_r
                im = term_i if im is None else im + term_i
            hops.append((re, im))
        for s in range(4):
            chi = s // 2
            same = (-hops[s][0], -hops[s][1])
            power = PHASE[direction][chi]
            if ODD_SIGN[direction] and s % 2 == 1:
                power = (power + 2) % 4
            cross = turn(*hops[SOURCE[direction][s]], power)
            of_real, of_imag = hop_rows(same, cross, chi)
            k = (s % 2) * 3 + c
            right[chi, 96 * slot:96 * slot + 96, 128 * k:128 * k + 128] = of_real
            right[chi, 96 * slot:96 * slot + 96, 128 * (k + 6):128 * (k + 7)] = of_imag


def place_left(values, mask_ref, left):
    copies = mask_ref.shape[0] // 48
    for s in range(4):
        for c in range(3):
            for q in range(2):
                part = values[s][c][q]
                twice = jnp.concatenate([part, part], 0).astype(jnp.bfloat16)
                k = q * 6 + (s % 2) * 3 + c
                for i in range(copies):
                    rows = slice(48 * i, 48 * i + 48)
                    left[s // 2, rows, 128 * k:128 * k + 128] = twice * mask_ref[rows, :]


def masks(mask_ref):
    rows = lax.broadcasted_iota(jnp.int32, mask_ref.shape, 0)
    lanes = lax.broadcasted_iota(jnp.int32, mask_ref.shape, 1)
    kind = rows // 192
    aggregate = rows % 192 // 24
    own = (lanes % LAT_X) // 4 == aggregate
    y_edge = lanes // LAT_X % 4 == 3
    x_edge = lanes % 4 == 3
    keep = own & ((kind == 0) | ((kind == 1) & y_edge) | ((kind == 2) & x_edge))
    mask_ref[...] = jnp.where(keep, 1.0, 0.0).astype(jnp.bfloat16)


def load(read):
    out = []
    for s in range(4):
        row = []
        for c in range(3):
            whole = read(s, c).astype(jnp.float32)
            row.append((whole[:24], whole[24:]))
        out.append(row)
    return out


def product(left, right):
    return lax.dot_general(left, right, (((1,), (1,)), ((), ())), preferred_element_type=jnp.float32)


def plane_kernel(v_ref, u_ref, sums, mask, left, right):
    masks(mask)
    sums[...] = jnp.zeros_like(sums)
    lane = lax.broadcasted_iota(jnp.int32, (24, 128), 1)
    wraps = lane % LAT_X == LAT_X - 1

    @pl.loop(0, v_ref.shape[0])
    def _(tz):
        values = load(lambda s, c: v_ref[tz, s, c])
        place_left(values, mask, left)
        for s in range(4):
            for c in range(3):
                vr, vi = values[s][c]
                k = (s % 2) * 3 + c
                right[s // 2, 192:240, 128 * k:128 * k + 128] = (
                    jnp.concatenate([vr, vi], 0).astype(jnp.bfloat16))
                right[s // 2, 192:240, 128 * (k + 6):128 * (k + 7)] = (
                    jnp.concatenate([vi, -vr], 0).astype(jnp.bfloat16))

        def ahead_y(part):
            return pltpu.roll(part, 128 - LAT_X, 1)

        def ahead_x(part):
            return jnp.where(wraps, pltpu.roll(part, LAT_X - 1, 1), pltpu.roll(part, 127, 1))

        for slot, (direction, move) in enumerate(((2, ahead_y), (3, ahead_x))):
            shifted = [[(move(values[s][c][0]), move(values[s][c][1])) for c in range(3)] for s in range(4)]
            place_hops(direction, slot, shifted, u_ref, tz, right)
        for chi in range(2):
            sums[chi] += product(left[chi], right[chi])


def line_kernel(v_ref, u_ref, face_t, face_z, plane_sums, blocks, mask, left, right, sums, held):
    masks(mask)
    sums[...] = jnp.zeros_like(sums)

    @pl.loop(0, v_ref.shape[0])
    def _(tz):
        t = tz // 4
        z = tz % 4

        @pl.when(t < 3)
        def _():
            held[0] = v_ref[jnp.minimum(tz + 4, 15)]

        @pl.when(t == 3)
        def _():
            held[0] = face_t[z]

        @pl.when(z < 3)
        def _():
            held[1] = v_ref[jnp.minimum(tz + 1, 15)]

        @pl.when(z == 3)
        def _():
            held[1] = face_z[t]

        values = load(lambda s, c: v_ref[tz, s, c])
        place_left(values, mask, left)
        for direction in range(2):
            shifted = load(lambda s, c: held[direction, s, c])
            place_hops(direction, direction, shifted, u_ref, tz, right)
        kind = jnp.where(t == 3, 2, 0) + jnp.where(z == 3, 1, 0)
        for chi in range(2):
            sums[kind, chi] += product(left[chi], right[chi])

    row = lax.broadcasted_iota(jnp.int32, (48, 48), 0)
    col = lax.broadcasted_iota(jnp.int32, (48, 48), 1)
    sign = jnp.where((row < 24) == (col < 24), 1.0, -1.0)
    zero = jnp.zeros((24, 24), jnp.float32)
    for a in range(8):
        parts = [[], [], [], [], []]
        for chi in range(2):
            rows = slice(24 * a, 24 * a + 24)
            k0, k1, k2, k3 = [sums[kind, chi, rows, :] for kind in range(4)]
            whole = plane_sums[chi, rows, :]
            y_out = plane_sums[chi, 192 + 24 * a:216 + 24 * a, 0:96]
            x_out = plane_sums[chi, 384 + 24 * a:408 + 24 * a, 96:192]
            t_out = (k2 + k3)[:, 0:96]
            z_out = (k1 + k3)[:, 96:192]
            inner = (k0 + k1)[:, 0:96] + (k0 + k2)[:, 96:192]
            inner = inner + (whole[:, 0:96] - y_out) + (whole[:, 96:192] - x_out)
            g_re, g_im = whole[:, 192:216], whole[:, 216:240]
            gram = [g_re, zero, g_im, zero] if chi == 0 else [zero, g_re, zero, g_im]
            for i, part in enumerate((inner, t_out, z_out, y_out, x_out)):
                parts[i].append(part)
            parts[0][chi] = (inner, jnp.concatenate(gram, 1))
        inner = jnp.concatenate([parts[0][0][0], parts[0][1][0]], 0)
        gram = jnp.concatenate([parts[0][0][1], parts[0][1][1]], 0)
        adj = jnp.concatenate([sign * inner[:, :48].T, -sign * inner[:, 48:].T], 1)
        blocks[a, 0] = gram + inner + adj
        for i in range(1, 5):
            blocks[a, i] = jnp.concatenate(parts[i], 0)


def coarse_kernel(axes, blocks, phi_ref, out_ref, phi, ahead, back, got, send, recv):
    counts = [lax.axis_size(name) for name in axes]
    here = [lax.axis_index(name) for name in axes]

    def target(axis, step):
        spot = list(here)
        spot[axis] = lax.rem(here[axis] + step + counts[axis], counts[axis])
        return tuple(spot)

    barrier = pltpu.get_barrier_semaphore()
    for axis in range(2):
        for step in (-1, 1):
            pl.semaphore_signal(barrier, inc=1, device_id=target(axis, step), device_id_type=MESH)
    pl.semaphore_wait(barrier, 4)

    lane = lax.broadcasted_iota(jnp.int32, (1, 96), 1)
    row48 = lax.broadcasted_iota(jnp.int32, (48, 96), 0)
    lane48 = lax.broadcasted_iota(jnp.int32, (48, 96), 1)
    first = lane < 48
    gamma_row = jnp.where(lane % 48 < 24, 1.0, -1.0)
    gamma_col = jnp.where(lax.broadcasted_iota(jnp.int32, (48, 1), 0) < 24, 1.0, -1.0)
    eye_re = jnp.where(row48 == lane48, 1.0, 0.0)
    eye_im = jnp.where(row48 + 48 == lane48, 1.0, 0.0)

    def swapped(vector):
        return jnp.concatenate([vector[:, 48:], vector[:, :48]], 1)

    def forward(block, vector):
        other = swapped(vector)
        return block * jnp.where(first, vector, -vector), block * other

    def columns(vector):
        re = jnp.sum(vector * eye_re, 1, keepdims=True) * gamma_col
        im = jnp.sum(vector * eye_im, 1, keepdims=True) * gamma_col
        return re, im

    def backward(block, cols):
        re = jnp.sum(block * cols[0], 0, keepdims=True)
        im = jnp.sum(block * cols[1], 0, keepdims=True)
        other_im = swapped(im)
        return gamma_row * jnp.where(first, re + other_im, other_im - re)

    def copy(step, kind, src, dst, to):
        return pltpu.make_async_remote_copy(
            src_ref=src, dst_ref=dst, send_sem=send.at[step, kind], recv_sem=recv.at[step, kind],
            device_id=to, device_id_type=MESH)

    phi[0] = phi_ref[...]
    for step in range(2):
        copies = []
        for axis in range(2):
            copies.append(copy(step, axis, phi.at[step], ahead.at[step, axis], target(axis, -1)))
            copies[-1].start()
        local = [None] * 8
        cols = [columns(phi[step, a:a + 1]) for a in range(8)]
        for axis in range(2):
            for a in range(8):
                back[step, axis, a:a + 1] = backward(blocks[a, 1 + axis], cols[a])
            copies.append(copy(step, 2 + axis, back.at[step, axis], got.at[step, axis], target(axis, 1)))
            copies[-1].start()
        sums = []
        rows = []
        for a in range(8):
            own = phi[step, a:a + 1]
            right = phi[step, (a + 1) % 8:(a + 1) % 8 + 1]
            re0, im0 = forward(blocks[a, 0] + blocks[a, 3], own)
            re1, im1 = forward(blocks[a, 4], right)
            sums.append((re0 + re1, im0 + im1))
            rows.append(backward(blocks[a, 3], cols[a]) + backward(blocks[(a + 7) % 8, 4], cols[(a + 7) % 8]))
        for item in copies:
            item.wait()
        for a in range(8):
            re, im = sums[a]
            for axis in range(2):
                more_re, more_im = forward(blocks[a, 1 + axis], ahead[step, axis, a:a + 1])
                re = re + more_re
                im = im + more_im
            re = jnp.sum(re, 1, keepdims=True)
            im = jnp.sum(im, 1, keepdims=True)
            total = jnp.sum(re * eye_re + im * eye_im, 0, keepdims=True) + rows[a]
            total = total + got[step, 0, a:a + 1] + got[step, 1, a:a + 1]
            if step == 0:
                phi[1, a:a + 1] = total
            else:
                out_ref[a:a + 1] = total


def shifted_2(value, axis, steps):
    count = lax.axis_size(axis)
    pairs = [(source, (source + steps) % count) for source in range(count)]
    return lax.ppermute(value, axis, pairs)


def per_device(null_vectors, gauge_links, coarse_in):
    vectors = null_vectors.reshape(2, 24, 4, 3, 16, 128).transpose(4, 2, 3, 0, 1, 5).reshape(16, 4, 3, 48, 128)
    links = gauge_links.reshape(72, 16, 128).transpose(1, 0, 2).astype(jnp.float32) * 0.5
    face_t = shifted_2(vectors[0:4], "ta", -1)
    face_z = shifted_2(vectors[0::4], "sa", -1)
    vmem = pl.BlockSpec(memory_space=pltpu.VMEM)
    limit = pltpu.CompilerParams(vmem_limit_bytes=48 * 1024 * 1024)
    plane_sums = pl.pallas_call(
        plane_kernel,
        out_shape=jax.ShapeDtypeStruct((2, 576, 240), jnp.float32),
        in_specs=[vmem] * 2,
        out_specs=vmem,
        scratch_shapes=[
            pltpu.VMEM((576, 128), jnp.bfloat16),
            pltpu.VMEM((2, 576, 1536), jnp.bfloat16),
            pltpu.VMEM((2, 240, 1536), jnp.bfloat16),
        ],
        compiler_params=limit,
        cost_estimate=pl.CostEstimate(flops=14_000_000_000, bytes_accessed=4_000_000, transcendentals=0),
    )(vectors, links)
    blocks = pl.pallas_call(
        line_kernel,
        out_shape=jax.ShapeDtypeStruct((8, 5, 48, 96), jnp.float32),
        in_specs=[vmem] * 5,
        out_specs=vmem,
        scratch_shapes=[
            pltpu.VMEM((192, 128), jnp.bfloat16),
            pltpu.VMEM((2, 192, 1536), jnp.bfloat16),
            pltpu.VMEM((2, 192, 1536), jnp.bfloat16),
            pltpu.VMEM((4, 2, 192, 192), jnp.float32),
            pltpu.VMEM((2, 4, 3, 48, 128), jnp.bfloat16),
        ],
        compiler_params=limit,
        cost_estimate=pl.CostEstimate(flops=6_000_000_000, bytes_accessed=6_000_000, transcendentals=0),
    )(vectors, links, face_t, face_z, plane_sums)
    rows = coarse_in.reshape(8, 96)
    out = pl.pallas_call(
        functools.partial(coarse_kernel, ("ta", "sa")),
        out_shape=jax.ShapeDtypeStruct((8, 96), jnp.float32),
        in_specs=[vmem] * 2,
        out_specs=vmem,
        scratch_shapes=[
            pltpu.VMEM((2, 8, 96), jnp.float32),
            pltpu.VMEM((2, 2, 8, 96), jnp.float32),
            pltpu.VMEM((2, 2, 8, 96), jnp.float32),
            pltpu.VMEM((2, 2, 8, 96), jnp.float32),
            pltpu.SemaphoreType.DMA((2, 4)),
            pltpu.SemaphoreType.DMA((2, 4)),
        ],
        compiler_params=pltpu.CompilerParams(
            collective_id=0, has_side_effects=True, vmem_limit_bytes=48 * 1024 * 1024),
    )(blocks, rows)
    stored = blocks.reshape(8, 5, 48, 2, 48).transpose(0, 1, 3, 2, 4).reshape(1, 1, 8, 5, 4608)
    return stored, out.reshape(1, 1, 8, 96)


def solution(mesh):
    placed = (
        P(None, None, None, None, "ta", "sa", None),
        P(None, None, None, None, "ta", "sa", None),
        P("ta", "sa", None, None),
    )
    return jax.shard_map(
        per_device,
        mesh=mesh,
        in_specs=placed,
        out_specs=(P("ta", "sa", None, None, None), P("ta", "sa", None, None)),
        check_vma=False,
    )
```

time: 849 us -> 70.4 us (0.08); the launches traced: 834 us -> 70.2 us
  local copies, waits for them, and re-layouts: 562 us -> 10.1 us
  other arithmetic: 165 us -> 0.13 us
  matrix products: 87.2 us -> 0 us
  Pallas kernels: 0 us -> 52.5 us
    gather x11 -> x0, local copies, waits for them, and re-layouts: 293 us -> none  [the longest x9 263 us: regroup(): picked = jnp.take(flat, order, axis=-1)]
    reshape x15 -> x3, local copies, waits for them, and re-layouts: 149 us -> 7.72 us  [the longest x2 4.53 us: per_device(): blocks.reshape(8, 5, 48, 2, 48).transpose(0, 1, 3, 2, 4)]
    dot_general x90 -> x0, matrix products: 87.2 us -> none  [the longest x72 60.6 us: times_vector(): jnp.einsum('...ij,...j->...i', matrix, column, precision=lax.Precision.HI...]
    select_n x4 -> x0, other arithmetic: 75.1 us -> none  [the longest x2 63.9 us: regroup(): picked = jnp.take(flat, order, axis=-1)]
    pallas_call x0 -> x3, Pallas kernels: none -> 52.5 us  [the longest x1 24.8 us: per_device(): pl.pallas_call(plane_kernel, out_shape=jax.ShapeDtypeStruct((2, 576, 240)...]
    another operation x15 -> x0, local copies, waits for them, and re-layouts: 30.2 us -> none  [the longest x4 22.9 us: regroup(): flat = field.reshape(leading + (depth * plane_size,))]
    concatenate x24 -> x0, other arithmetic: 29.2 us -> none  [the longest x14 13.4 us: contract_agg(): return jnp.concatenate(row_blocks, axis=-2)]
    unnamed x197 -> x7, local copies, waits for them, and re-layouts: 28 us -> 0.61 us
  transfers between devices with their start and end apart: 10 -> 2, of which waited for: 1 -> 0; matrix products, arithmetic and copies ran while one was open for 95% -> 1% of each run, Pallas kernels for 0% -> 35%
where the time goes in v1:
time: 70.4 us; the launch traced here: 70.2 us
  Pallas kernels  52.5 us (75%)
  local copies, waits for them, and re-layouts  10.1 us (14%)
  starting transfers between devices  6.76 us (10%)
  between operations  0.74 us (1%)
    pallas_call x1, Pallas kernels, per_device(): pl.pallas_call(plane_kernel, out_shape=jax.ShapeDtypeStruct((2, 576, 240)...  24.8 us
    pallas_call x1, Pallas kernels, per_device(): pl.pallas_call(line_kernel, out_shape=jax.ShapeDtypeStruct((8, 5, 48, 96)...  18.1 us
    pallas_call x1, Pallas kernels, per_device(): pl.pallas_call(functools.partial(coarse_kernel, ('ta', 'sa')), out_shape=...  9.54 us
    ppermute x2, starting transfers between devices, shifted_2(): return lax.ppermute(value, axis, pairs)  6.76 us
    reshape x2, local copies, waits for them, and re-layouts, per_device(): blocks.reshape(8, 5, 48, 2, 48).transpose(0, 1, 3, 2, 4)  4.53 us
    reshape x1, local copies, waits for them, and re-layouts, per_device(): null_vectors.reshape(2, 24, 4, 3, 16, 128).transpose(4, 2, 3, 0, 1, 5)  3.19 us
    transpose x1, local copies, waits for them, and re-layouts, per_device(): blocks.reshape(8, 5, 48, 2, 48).transpose(0, 1, 3, 2, 4)  1.45 us
  transfers between devices with their start and end apart: 2, of which 0 were waited for; matrix products, arithmetic and copies ran while one was open for 1% of the time, Pallas kernels for 35%

profile of v1, /device:TPU:0, one launch (start us, length us, event | category | flops | bytes accessed | tf_op | source)
XLA Modules:
  0.0 70.2 jit_solution(8553933938597885247)
XLA Ops:
  0.6 3.2 %copy.15 = bf16[2,24,4,3,16,128]{5,1,0,3,2,4:T(8,128)(2,1)S(1)} copy(bf16[2,24,4,3,16,128]{5,4,3,2,1,0:T(8,128)(2,1)} %bitcast.29) | data formatting | bytes 4718592 | tf_op jit(solution)/shard_map/reshape | solution.py:295
  3.8 0.0 copy-start
  3.8 0.0 copy-start.2
  3.9 5.1 %collective-permute-start.1 = (bf16[4,4,3,48,128]{4,3,2,1,0:T(8,128)(2,1)S(1)}, bf16[4,4,3,48,128]{4,3,2,1,0:T(8,128)(2,1)S(1)}, u32[]{:S(2)}, u32[]{:S(2)}) collective-permute-start(bf16[4,4,3,48,128]{4,3,2,1,0:T(8,128)(2,1)S(1)} %slice.11), channel_id=1, source_target_pairs={{0,3},{1,0},{2,1},{3,2},{4,7},{5,4},{6,5},{7,6},{8,11},{9,8},{10,9... | collective-permute-start | bytes 1769480 | tf_op jit(solution)/shard_map/ppermute | solution.py:291
  9.0 0.1 slice.12
  9.1 1.7 %collective-permute-start = (bf16[4,4,3,48,128]{4,3,2,1,0:T(8,128)(2,1)S(1)}, bf16[4,4,3,48,128]{4,3,2,1,0:T(8,128)(2,1)S(1)}, u32[]{:S(2)}, u32[]{:S(2)}) collective-permute-start(bf16[4,4,3,48,128]{4,3,2,1,0:T(8,128)(2,1)S(1)} %bitcast.31), channel_id=1, source_target_pairs={{0,28},{4,0},{8,4},{12,8},{16,12},{20,16},{24,20},{28,24},{1,29},{... | collective-permute-start | bytes 1769480 | tf_op jit(solution)/shard_map/ppermute | solution.py:291
  10.7 0.0 copy-done.2
  10.7 0.1 convert_multiply_fusion
  10.8 0.2 copy.14
  11.0 0.0 copy-done
  11.1 24.8 %shard_map.50.plane_sums = f32[2,576,240]{2,1,0:T(8,128)S(1)} custom-call(bf16[16,4,3,48,128]{4,3,2,1,0:T(8,128)(2,1)S(1)} %bitcast.22, f32[16,72,128]{2,1,0:T(8,128)S(1)} %bitcast.24), custom_call_target="tpu_custom_call" | custom-call | flops 14000000000 | bytes 4000000 | tf_op jit(solution)/shard_map/pallas_call | solution.py:301
  35.9 0.0 collective-permute-done.1.face_z
  35.9 0.0 collective-permute-done.face_t
  35.9 18.1 %shard_map.51.blocks = f32[8,5,48,96]{3,2,1,0:T(8,128)S(1)} custom-call(bf16[16,4,3,48,128]{4,3,2,1,0:T(8,128)(2,1)} %bitcast.23, f32[16,72,128]{2,1,0:T(8,128)S(1)} %bitcast.25, bf16[4,4,3,48,128]{4,3,2,1,0:T(8,128)(2,1)S(1)} %collective-permute-done.face_t, bf16[4,4,3,48,128]{4,3,2,1,0:T(8,128)(2,1)S(1)} %collective-permute-done.1.face_z, ...), custom_call_target="tpu_custom_call" | custom-call | flops 6000000000 | bytes 6000000 | tf_op jit(solution)/shard_map/pallas_call | solution.py:314
  54.0 0.0 copy-start.1
  54.0 1.1 %reshape.29 = f32[8,5,48,2,48]{4,3,2,1,0:T(2,128)S(1)} reshape(f32[8,5,48,96]{3,2,1,0:T(8,128)S(1)} %shard_map.51.blocks) | data formatting | bytes 1474560 | tf_op jit(solution)/shard_map/reshape | solution.py:346
  55.1 0.0 copy-done.1
  55.1 9.5 %shard_map.52 = f32[8,96]{1,0:T(8,128)S(1)} custom-call(f32[8,5,48,96]{3,2,1,0:T(8,128)S(1)} %shard_map.51.blocks, f32[8,96]{1,0:T(8,128)S(1)} %bitcast.27), custom_call_target="tpu_custom_call" | custom-call | tf_op jit(solution)/shard_map/pallas_call | solution.py:330
  64.7 1.4 %copy.10 = f32[8,5,2,48,48]{4,3,2,0,1:T(8,128)} copy(f32[8,5,2,48,48]{4,2,3,1,0:T(2,128)S(1)} %bitcast.28) | data formatting | bytes 1474560 | tf_op jit(solution)/shard_map/transpose | solution.py:346
  66.1 3.4 %reshape.30 = f32[1,1,8,5,4608]{4,2,3,1,0:T(8,128)} reshape(f32[8,5,2,48,48]{4,3,2,0,1:T(8,128)} %copy.10) | data formatting | bytes 1474560 | tf_op jit(solution)/shard_map/reshape | solution.py:346
  69.6 0.6 copy.17
  (1 shorter events, 0.0 us)
Async XLA Ops:
  3.8 7.2 %copy-start = (bf16[2,24,4,3,16,128]{5,1,0,3,2,4:T(8,128)(2,1)}, bf16[2,24,4,3,16,128]{5,1,0,3,2,4:T(8,128)(2,1)S(1)}, u32[]{:S(2)}) copy-start(bf16[2,24,4,3,16,128]{5,1,0,3,2,4:T(8,128)(2,1)S(1)} %copy.15) | copy-start | bytes 7077892
  3.8 6.9 %copy-start.2 = (bf16[2,4,3,3,4,4,128]{6,5,4,3,2,1,0:T(4,128)(2,1)S(1)}, bf16[2,4,3,3,4,4,128]{6,5,4,3,2,1,0:T(4,128)(2,1)}, u32[]{:S(2)}) copy-start(bf16[2,4,3,3,4,4,128]{6,5,4,3,2,1,0:T(4,128)(2,1)} %param.4) | copy-start | bytes 884740
  3.9 32.0 %collective-permute-start.1 = (bf16[4,4,3,48,128]{4,3,2,1,0:T(8,128)(2,1)S(1)}, bf16[4,4,3,48,128]{4,3,2,1,0:T(8,128)(2,1)S(1)}, u32[]{:S(2)}, u32[]{:S(2)}) collective-permute-start(bf16[4,4,3,48,128]{4,3,2,1,0:T(8,128)(2,1)S(1)} %slice.11), channel_id=1, source_target_pairs={{0,3},{1,0},{2,1},{3,2},{4,7},{5,4},{6,5},{7,6},{8,11},{9,8},{10,9... | collective-permute-start | bytes 1769480 | tf_op jit(solution)/shard_map/ppermute | solution.py:291
  9.1 26.8 %collective-permute-start = (bf16[4,4,3,48,128]{4,3,2,1,0:T(8,128)(2,1)S(1)}, bf16[4,4,3,48,128]{4,3,2,1,0:T(8,128)(2,1)S(1)}, u32[]{:S(2)}, u32[]{:S(2)}) collective-permute-start(bf16[4,4,3,48,128]{4,3,2,1,0:T(8,128)(2,1)S(1)} %bitcast.31), channel_id=1, source_target_pairs={{0,28},{4,0},{8,4},{12,8},{16,12},{20,16},{24,20},{28,24},{1,29},{... | collective-permute-start | bytes 1769480 | tf_op jit(solution)/shard_map/ppermute | solution.py:291
  54.0 1.1 %copy-start.1 = (f32[1,1,8,96]{3,2,1,0:T(8,128)S(1)}, f32[1,1,8,96]{3,2,1,0:T(8,128)}, u32[]{:S(2)}) copy-start(f32[1,1,8,96]{3,2,1,0:T(8,128)} %param.5) | copy-start | bytes 9220

commit v2 on v1

v2 whole, which is shorter than its diff:
```python
import functools

import jax
import jax.numpy as jnp
from jax import lax
from jax.experimental import pallas as pl
from jax.experimental.pallas import tpu as pltpu
from jax.sharding import PartitionSpec as P

LAT_X = 32
MESH = pl.DeviceIdType.MESH

SOURCE = ((2, 3, 0, 1), (2, 3, 0, 1), (3, 2, 1, 0), (3, 2, 1, 0))
ODD_SIGN = (False, True, True, False)
PHASE = ((0, 0), (3, 1), (2, 0), (3, 1))


def turn(re, im, power):
    if power == 0:
        return re, im
    if power == 1:
        return -im, re
    if power == 2:
        return -re, -im
    return im, -re


def hop_rows(same, cross, chi):
    first, second = (same, cross) if chi == 0 else (cross, same)
    of_real = jnp.concatenate([first[0], second[0], first[1], second[1]], 0)
    of_imag = jnp.concatenate([first[1], second[1], -first[0], -second[0]], 0)
    return of_real.astype(jnp.bfloat16), of_imag.astype(jnp.bfloat16)


def place_hops(direction, slot, shifted, u_ref, a, h, right):
    links = []
    for q in range(2):
        links.append([[u_ref[a, h, pl.ds(((q * 4 + direction) * 3 + row) * 3 + col, 1), :]
                       for col in range(3)] for row in range(3)])
    for c in range(3):
        hops = []
        for s in range(4):
            re = None
            im = None
            for d in range(3):
                lr, li = links[0][c][d], links[1][c][d]
                vr, vi = shifted[s][d]
                term_r = lr * vr - li * vi
                term_i = lr * vi + li * vr
                re = term_r if re is None else re + term_r
                im = term_i if im is None else im + term_i
            hops.append((re, im))
        for s in range(4):
            chi = s // 2
            same = (-hops[s][0], -hops[s][1])
            power = PHASE[direction][chi]
            if ODD_SIGN[direction] and s % 2 == 1:
                power = (power + 2) % 4
            cross = turn(*hops[SOURCE[direction][s]], power)
            of_real, of_imag = hop_rows(same, cross, chi)
            k = (s % 2) * 3 + c
            right[chi, 96 * slot:96 * slot + 96, 128 * k:128 * k + 128] = of_real
            right[chi, 96 * slot:96 * slot + 96, 128 * (k + 6):128 * (k + 7)] = of_imag


def place_left(values, edges, left):
    for s in range(4):
        for c in range(3):
            for q in range(2):
                part = values[s][c][q]
                zero = jnp.zeros_like(part)
                rows = [part, jnp.where(edges[0], part, zero), jnp.where(edges[1], part, zero), zero]
                k = q * 6 + (s % 2) * 3 + c
                left[s // 2, :, 128 * k:128 * k + 128] = jnp.concatenate(rows, 0).astype(jnp.bfloat16)


def load(ref, *index):
    out = []
    for s in range(4):
        row = []
        for c in range(3):
            k = 48 * (s * 3 + c)
            whole = ref[*index, k:k + 48, :].astype(jnp.float32)
            row.append((whole[:24], whole[24:]))
        out.append(row)
    return out


def moved(move, *fields):
    return [[tuple(move(*(f[s][c][q] for f in fields)) for q in range(2)) for c in range(3)] for s in range(4)]


def product(left, right):
    return lax.dot_general(left, right, (((1,), (1,)), ((), ())), preferred_element_type=jnp.float32)


def spread_kernel(v_ref, u_ref, v_out, u_out, place):
    row = lax.broadcasted_iota(jnp.int32, (128, 1024), 0)
    col = lax.broadcasted_iota(jnp.int32, (128, 1024), 1)
    hit = row == col % 16 // 4 * LAT_X + col // 128 * 4 + col % 4
    for k in range(8):
        place[128 * k:128 * k + 128, :] = jnp.where(hit & (col % 128 // 16 == k), 1.0, 0.0).astype(jnp.bfloat16)
    for h in range(2):
        for ref, out in ((v_ref, v_out), (u_ref, u_out)):
            wide = jnp.concatenate([ref[8 * h + k] for k in range(8)], 1)
            found = jnp.dot(wide, place[...], preferred_element_type=jnp.float32)
            for a in range(8):
                part = found[:, 128 * a:128 * a + 128]
                out[a, h] = part.astype(jnp.bfloat16) if ref is v_ref else 0.5 * part


def plane_kernel(v_ref, u_ref, sums, left0, left1, right0, right1):
    lane = lax.broadcasted_iota(jnp.int32, (24, 128), 1)
    y_edge = lane // 4 % 4 == 3
    x_edge = lane % 4 == 3

    def ahead_y(part):
        return jnp.where(y_edge, pltpu.roll(part, 12, 1), pltpu.roll(part, 124, 1))

    def ahead_x(part, following):
        return jnp.where(x_edge, pltpu.roll(following, 3, 1), pltpu.roll(part, 127, 1))

    @pl.loop(0, 8)
    def _(a):
        after = lax.rem(a + 1, 8)
        for h, (left, right) in enumerate(((left0, right0), (left1, right1))):
            values = load(v_ref, a, h)
            place_left(values, (y_edge, x_edge), left)
            for s in range(4):
                for c in range(3):
                    vr, vi = values[s][c]
                    k = (s % 2) * 3 + c
                    right[s // 2, 192:240, 128 * k:128 * k + 128] = (
                        jnp.concatenate([vr, vi], 0).astype(jnp.bfloat16))
                    right[s // 2, 192:240, 128 * (k + 6):128 * (k + 7)] = (
                        jnp.concatenate([vi, -vr], 0).astype(jnp.bfloat16))
            place_hops(2, 0, moved(ahead_y, values), u_ref, a, h, right)
            place_hops(3, 1, moved(ahead_x, values, load(v_ref, after, h)), u_ref, a, h, right)
        for chi in range(2):
            sums[a, chi] = product(right0[chi], left0[chi]) + product(right1[chi], left1[chi])


def line_kernel(v_ref, u_ref, face_t, face_z, place, plane_sums, blocks, stored,
                far_t, far_z, left0, left1, right0, right1):
    wide = jnp.concatenate([face_t[k] for k in range(4)], 1)
    found = jnp.dot(wide, place[0:512, :], preferred_element_type=jnp.float32)
    for a in range(8):
        far_t[a] = found[:, 128 * a:128 * a + 128].astype(jnp.bfloat16)
    ends = jnp.concatenate([place[384:512, :], place[896:1024, :]], 0)
    for h in range(2):
        wide = jnp.concatenate([face_z[2 * h], face_z[2 * h + 1]], 1)
        found = jnp.dot(wide, ends, preferred_element_type=jnp.float32)
        for a in range(8):
            far_z[a, h] = found[:, 128 * a:128 * a + 128].astype(jnp.bfloat16)

    lane = lax.broadcasted_iota(jnp.int32, (24, 128), 1)
    upper = lane >= 64
    z_edge = lane // 16 % 4 == 3
    nowhere = lane < 0
    row = lax.broadcasted_iota(jnp.int32, (48, 48), 0)
    col = lax.broadcasted_iota(jnp.int32, (48, 48), 1)
    sign = jnp.where((row < 24) == (col < 24), 1.0, -1.0)
    zero = jnp.zeros((24, 24), jnp.float32)

    def ahead_t(part, following):
        return pltpu.roll(jnp.where(upper, part, following), 64, 1)

    def ahead_z(part, face):
        return jnp.where(z_edge, face, pltpu.roll(part, 112, 1))

    @pl.loop(0, 8)
    def _(a):
        for h, (left, right) in enumerate(((left0, right0), (left1, right1))):
            values = load(v_ref, a, h)
            place_left(values, (upper if h == 1 else nowhere, z_edge), left)
            following = load(v_ref, a, 1) if h == 0 else load(far_t, a)
            place_hops(0, 0, moved(ahead_t, values, following), u_ref, a, h, right)
            place_hops(1, 1, moved(ahead_z, values, load(far_z, a, h)), u_ref, a, h, right)
        line = []
        plane = []
        for chi in range(2):
            line.append(product(right0[chi], left0[chi]) + product(right1[chi], left1[chi]))
            plane.append(plane_sums[a, chi])

        def pick(sums, slot, kind):
            return jnp.concatenate(
                [part[96 * slot:96 * slot + 96, 24 * kind:24 * kind + 24] for part in sums], 1)

        inner = (pick(line, 0, 0) - pick(line, 0, 1)) + (pick(line, 1, 0) - pick(line, 1, 2))
        inner = inner + (pick(plane, 0, 0) - pick(plane, 0, 1)) + (pick(plane, 1, 0) - pick(plane, 1, 2))
        gram = []
        for part in range(2):
            rows = slice(192 + 24 * part, 216 + 24 * part)
            gram.append(jnp.concatenate([plane[0][rows, 0:24], zero], 1))
            gram.append(jnp.concatenate([zero, plane[1][rows, 0:24]], 1))
        whole = (inner + jnp.concatenate(gram, 0)).T
        whole = whole + jnp.concatenate([sign * inner[:48], -sign * inner[48:]], 1)
        kept = [whole, pick(line, 0, 1).T, pick(line, 1, 2).T, pick(plane, 0, 1).T, pick(plane, 1, 2).T]
        for i, block in enumerate(kept):
            blocks[a, i] = block
            stored[a, i, 0] = block[:, :48]
            stored[a, i, 1] = block[:, 48:]


def coarse_kernel(axes, blocks, phi_ref, out_ref, phi, ahead, back, got, send, recv):
    counts = [lax.axis_size(name) for name in axes]
    here = [lax.axis_index(name) for name in axes]

    def target(axis, step):
        spot = list(here)
        spot[axis] = lax.rem(here[axis] + step + counts[axis], counts[axis])
        return tuple(spot)

    barrier = pltpu.get_barrier_semaphore()
    for axis in range(2):
        for step in (-1, 1):
            pl.semaphore_signal(barrier, inc=1, device_id=target(axis, step), device_id_type=MESH)
    pl.semaphore_wait(barrier, 4)

    lane = lax.broadcasted_iota(jnp.int32, (1, 96), 1)
    row48 = lax.broadcasted_iota(jnp.int32, (48, 96), 0)
    lane48 = lax.broadcasted_iota(jnp.int32, (48, 96), 1)
    first = lane < 48
    gamma_row = jnp.where(lane % 48 < 24, 1.0, -1.0)
    gamma_col = jnp.where(lax.broadcasted_iota(jnp.int32, (48, 1), 0) < 24, 1.0, -1.0)
    eye_re = jnp.where(row48 == lane48, 1.0, 0.0)
    eye_im = jnp.where(row48 + 48 == lane48, 1.0, 0.0)

    def swapped(vector):
        return jnp.concatenate([vector[:, 48:], vector[:, :48]], 1)

    def forward(block, vector):
        other = swapped(vector)
        return block * jnp.where(first, vector, -vector), block * other

    def columns(vector):
        re = jnp.sum(vector * eye_re, 1, keepdims=True) * gamma_col
        im = jnp.sum(vector * eye_im, 1, keepdims=True) * gamma_col
        return re, im

    def backward(block, cols):
        re = jnp.sum(block * cols[0], 0, keepdims=True)
        im = jnp.sum(block * cols[1], 0, keepdims=True)
        other_im = swapped(im)
        return gamma_row * jnp.where(first, re + other_im, other_im - re)

    def copy(step, kind, src, dst, to):
        return pltpu.make_async_remote_copy(
            src_ref=src, dst_ref=dst, send_sem=send.at[step, kind], recv_sem=recv.at[step, kind],
            device_id=to, device_id_type=MESH)

    phi[0] = phi_ref[...]
    for step in range(2):
        copies = []
        for axis in range(2):
            copies.append(copy(step, axis, phi.at[step], ahead.at[step, axis], target(axis, -1)))
            copies[-1].start()
        local = [None] * 8
        cols = [columns(phi[step, a:a + 1]) for a in range(8)]
        for axis in range(2):
            for a in range(8):
                back[step, axis, a:a + 1] = backward(blocks[a, 1 + axis], cols[a])
            copies.append(copy(step, 2 + axis, back.at[step, axis], got.at[step, axis], target(axis, 1)))
            copies[-1].start()
        sums = []
        rows = []
        for a in range(8):
            own = phi[step, a:a + 1]
            right = phi[step, (a + 1) % 8:(a + 1) % 8 + 1]
            re0, im0 = forward(blocks[a, 0] + blocks[a, 3], own)
            re1, im1 = forward(blocks[a, 4], right)
            sums.append((re0 + re1, im0 + im1))
            rows.append(backward(blocks[a, 3], cols[a]) + backward(blocks[(a + 7) % 8, 4], cols[(a + 7) % 8]))
        for item in copies:
            item.wait()
        for a in range(8):
            re, im = sums[a]
            for axis in range(2):
                more_re, more_im = forward(blocks[a, 1 + axis], ahead[step, axis, a:a + 1])
                re = re + more_re
                im = im + more_im
            re = jnp.sum(re, 1, keepdims=True)
            im = jnp.sum(im, 1, keepdims=True)
            total = jnp.sum(re * eye_re + im * eye_im, 0, keepdims=True) + rows[a]
            total = total + got[step, 0, a:a + 1] + got[step, 1, a:a + 1]
            if step == 0:
                phi[1, a:a + 1] = total
            else:
                out_ref[a:a + 1] = total


def shifted_2(value, axis, steps):
    count = lax.axis_size(axis)
    pairs = [(source, (source + steps) % count) for source in range(count)]
    return lax.ppermute(value, axis, pairs)


def per_device(null_vectors, gauge_links, coarse_in):
    vectors = null_vectors.reshape(2, 24, 4, 3, 16, 128).transpose(4, 2, 3, 0, 1, 5).reshape(16, 576, 128)
    links = gauge_links.reshape(72, 16, 128).transpose(1, 0, 2)
    face_t = shifted_2(vectors[0:4], "ta", -1)
    face_z = shifted_2(vectors[0::4], "sa", -1)
    vmem = pl.BlockSpec(memory_space=pltpu.VMEM)
    limit = pltpu.CompilerParams(vmem_limit_bytes=48 * 1024 * 1024)
    spread_v, spread_u, place = pl.pallas_call(
        spread_kernel,
        out_shape=(
            jax.ShapeDtypeStruct((8, 2, 576, 128), jnp.bfloat16),
            jax.ShapeDtypeStruct((8, 2, 72, 128), jnp.float32),
            jax.ShapeDtypeStruct((1024, 1024), jnp.bfloat16),
        ),
        in_specs=[vmem] * 2,
        out_specs=(vmem, vmem, vmem),
        compiler_params=limit,
        cost_estimate=pl.CostEstimate(flops=2_700_000_000, bytes_accessed=7_000_000, transcendentals=0),
    )(vectors, links)
    operands = [
        pltpu.VMEM((2, 96, 1536), jnp.bfloat16),
        pltpu.VMEM((2, 96, 1536), jnp.bfloat16),
    ]
    plane_sums = pl.pallas_call(
        plane_kernel,
        out_shape=jax.ShapeDtypeStruct((8, 2, 240, 96), jnp.float32),
        in_specs=[vmem] * 2,
        out_specs=vmem,
        scratch_shapes=operands + [pltpu.VMEM((2, 240, 1536), jnp.bfloat16)] * 2,
        compiler_params=limit,
        cost_estimate=pl.CostEstimate(flops=8_000_000_000, bytes_accessed=4_000_000, transcendentals=0),
    )(spread_v, spread_u)
    blocks, stored = pl.pallas_call(
        line_kernel,
        out_shape=(
            jax.ShapeDtypeStruct((8, 5, 48, 96), jnp.float32),
            jax.ShapeDtypeStruct((8, 5, 2, 48, 48), jnp.float32),
        ),
        in_specs=[vmem] * 6,
        out_specs=(vmem, vmem),
        scratch_shapes=[
            pltpu.VMEM((8, 576, 128), jnp.bfloat16),
            pltpu.VMEM((8, 2, 576, 128), jnp.bfloat16),
        ] + operands + [pltpu.VMEM((2, 192, 1536), jnp.bfloat16)] * 2,
        compiler_params=limit,
        cost_estimate=pl.CostEstimate(flops=8_000_000_000, bytes_accessed=6_000_000, transcendentals=0),
    )(spread_v, spread_u, face_t, face_z, place, plane_sums)
    rows = coarse_in.reshape(8, 96)
    out = pl.pallas_call(
        functools.partial(coarse_kernel, ("ta", "sa")),
        out_shape=jax.ShapeDtypeStruct((8, 96), jnp.float32),
        in_specs=[vmem] * 2,
        out_specs=vmem,
        scratch_shapes=[
            pltpu.VMEM((2, 8, 96), jnp.float32),
            pltpu.VMEM((2, 2, 8, 96), jnp.float32),
            pltpu.VMEM((2, 2, 8, 96), jnp.float32),
            pltpu.VMEM((2, 2, 8, 96), jnp.float32),
            pltpu.SemaphoreType.DMA((2, 4)),
            pltpu.SemaphoreType.DMA((2, 4)),
        ],
        compiler_params=pltpu.CompilerParams(
            collective_id=0, has_side_effects=True, vmem_limit_bytes=48 * 1024 * 1024),
    )(blocks, rows)
    stored = stored.reshape(1, 1, 8, 5, 4608)
    return stored, out.reshape(1, 1, 8, 96)


def solution(mesh):
    placed = (
        P(None, None, None, None, "ta", "sa", None),
        P(None, None, None, None, "ta", "sa", None),
        P("ta", "sa", None, None),
    )
    return jax.shard_map(
        per_device,
        mesh=mesh,
        in_specs=placed,
        out_specs=(P("ta", "sa", None, None, None), P("ta", "sa", None, None)),
        check_vma=False,
    )
```

time: 70.4 us -> 64 us (0.909)
  Pallas kernels: 52.5 us -> 44.8 us
  local copies, waits for them, and re-layouts: 10.1 us -> 11.5 us
    pallas_call x2 -> x3, Pallas kernels: 42.9 us -> 35.3 us  [the longest x1 17.4 us: per_device(): pl.pallas_call(line_kernel, out_shape=(jax.ShapeDtypeStruct((8, 5, 48, 96...]
    unnamed x7 -> x13, local copies, waits for them, and re-layouts: 0.61 us -> 3.22 us
    transpose x1 -> x0, local copies, waits for them, and re-layouts: 1.45 us -> none  [per_device(): blocks.reshape(8, 5, 48, 2, 48).transpose(0, 1, 3, 2, 4)]
    reshape x2 -> x3, local copies, waits for them, and re-layouts: 4.53 us -> 4.99 us  [the longest x2 4.91 us: per_device(): stored = stored.reshape(1, 1, 8, 5, 4608)]
  transfers between devices with their start and end apart: 2 -> 2, of which waited for: 0 -> 0; matrix products, arithmetic and copies ran while one was open for 1% -> 0% of each run, Pallas kernels for 35% -> 28%
where the time goes in v2:
time: 64 us; the launch traced here: 63.8 us
  Pallas kernels  44.8 us (70%)
  local copies, waits for them, and re-layouts  11.5 us (18%)
  starting transfers between devices  6.76 us (11%)
  between operations  0.72 us (1%)
    pallas_call x1, Pallas kernels, per_device(): pl.pallas_call(line_kernel, out_shape=(jax.ShapeDtypeStruct((8, 5, 48, 96...  17.4 us
    pallas_call x1, Pallas kernels, per_device(): pl.pallas_call(plane_kernel, out_shape=jax.ShapeDtypeStruct((8, 2, 240, 9...  12.9 us
    pallas_call x1, Pallas kernels, per_device(): pl.pallas_call(functools.partial(coarse_kernel, ('ta', 'sa')), out_shape=...  9.48 us
    ppermute x2, starting transfers between devices, shifted_2(): return lax.ppermute(value, axis, pairs)  6.76 us
    pallas_call x1, Pallas kernels, per_device(): pl.pallas_call(spread_kernel, out_shape=(jax.ShapeDtypeStruct((8, 2, 576,...  5.04 us
    reshape x2, local copies, waits for them, and re-layouts, per_device(): stored = stored.reshape(1, 1, 8, 5, 4608)  4.91 us
    unnamed x13, local copies, waits for them, and re-layouts  3.22 us
    reshape x1, local copies, waits for them, and re-layouts, per_device(): null_vectors.reshape(2, 24, 4, 3, 16, 128).transpose(4, 2, 3, 0, 1, 5)  3.19 us
  transfers between devices with their start and end apart: 2, of which 0 were waited for; matrix products, arithmetic and copies ran while one was open for 0% of the time, Pallas kernels for 28%

profile of v2, /device:TPU:0, one launch (start us, length us, event | category | flops | bytes accessed | tf_op | source)
XLA Modules:
  0.0 63.8 jit_solution(9325487309117148141)
XLA Ops:
  0.6 3.2 %copy.16 = bf16[2,24,4,3,16,128]{5,1,0,3,2,4:T(8,128)(2,1)S(1)} copy(bf16[2,24,4,3,16,128]{5,4,3,2,1,0:T(8,128)(2,1)} %bitcast.21) | data formatting | bytes 4718592 | tf_op jit(solution)/shard_map/reshape | solution.py:299
  3.8 0.0 copy-start.4
  3.8 0.0 copy-start.5
  3.9 5.1 %collective-permute-start.1 = (bf16[4,576,128]{2,1,0:T(8,128)(2,1)S(1)}, bf16[4,576,128]{2,1,0:T(8,128)(2,1)S(1)}, u32[]{:S(2)}, u32[]{:S(2)}) collective-permute-start(bf16[4,576,128]{2,1,0:T(8,128)(2,1)S(1)} %slice.11), channel_id=1, source_target_pairs={{0,3},{1,0},{2,1},{3,2},{4,7},{5,4},{6,5},{7,6},{8,11},{9,8},{10,9... | collective-permute-start | bytes 1769480 | tf_op jit(solution)/shard_map/ppermute | solution.py:295
  9.0 0.1 slice.12
  9.1 1.7 %collective-permute-start = (bf16[4,576,128]{2,1,0:T(8,128)(2,1)S(1)}, bf16[4,576,128]{2,1,0:T(8,128)(2,1)S(1)}, u32[]{:S(2)}, u32[]{:S(2)}) collective-permute-start(bf16[4,576,128]{2,1,0:T(8,128)(2,1)S(1)} %bitcast.22), channel_id=1, source_target_pairs={{0,28},{4,0},{8,4},{12,8},{16,12},{20,16},{24,20},{28,24},{1,29},{... | collective-permute-start | bytes 1769480 | tf_op jit(solution)/shard_map/ppermute | solution.py:295
  10.7 0.0 copy-done.5
  10.7 0.1 copy.15
  10.8 0.0 copy-done.4
  10.8 5.0 %shard_map.50 = (bf16[8,2,576,128]{3,2,1,0:T(8,128)(2,1)S(1)}, f32[8,2,72,128]{3,2,1,0:T(8,128)S(1)}, bf16[1024,1024]{1,0:T(8,128)(2,1)S(1)}) custom-call(bf16[16,576,128]{2,1,0:T(8,128)(2,1)} %bitcast.20, bf16[16,72,128]{2,1,0:T(8,128)(2,1)S(1)} %bitcast.15), custom_call_target="tpu_custom_call" | custom-call | flops 2700000000 | bytes 7000000 | tf_op jit(solution)/shard_map/pallas_call | solution.py:305
  15.8 0.0 copy-start.2
  15.9 1.3 %copy-done.2 = bf16[1024,1024]{1,0:T(8,128)(2,1)} copy-done((bf16[1024,1024]{1,0:T(8,128)(2,1)}, bf16[1024,1024]{1,0:T(8,128)(2,1)S(1)}, u32[]{:S(2)}) %copy-start.2) | copy-done | bytes 2097176
  17.2 12.9 %shard_map.51.plane_sums = f32[8,2,240,96]{3,2,1,0:T(8,128)S(1)} custom-call(bf16[8,2,576,128]{3,2,1,0:T(8,128)(2,1)S(1)} %get-tuple-element.7.v_ref, f32[8,2,72,128]{3,2,1,0:T(8,128)S(1)} %get-tuple-element.8.u_ref), custom_call_target="tpu_custom_call" | custom-call | flops 8000000000 | bytes 4000000 | tf_op jit(solution)/shard_map/pallas_call | solution.py:321
  30.1 0.0 copy-done.1
  30.1 0.0 copy-start.3
  30.1 1.3 %copy-done.3 = f32[8,2,240,96]{3,2,1,0:T(8,128)} copy-done((f32[8,2,240,96]{3,2,1,0:T(8,128)}, f32[8,2,240,96]{3,2,1,0:T(8,128)S(1)}, u32[]{:S(2)}) %copy-start.3) | copy-done | bytes 1474584
  31.4 0.0 collective-permute-done.1.face_z
  31.4 0.0 collective-permute-done.face_t
  31.4 17.4 %shard_map.52 = (f32[8,5,48,96]{3,2,1,0:T(8,128)S(1)}, f32[8,5,2,48,48]{4,3,2,1,0:T(8,128)S(1)}) custom-call(bf16[8,2,576,128]{3,2,1,0:T(8,128)(2,1)} %copy-done.1, f32[8,2,72,128]{3,2,1,0:T(8,128)S(1)} %get-tuple-element.8.u_ref, bf16[4,576,128]{2,1,0:T(8,128)(2,1)S(1)} %collective-permute-done.face_t, ...), custom_call_target="tpu_custom_call" | custom-call | flops 8000000000 | bytes 6000000 | tf_op jit(solution)/shard_map/pallas_call | solution.py:330
  48.8 2.4 %reshape.29 = f32[1,1,8,5,4608]{4,3,2,1,0:T(8,128)} reshape(f32[8,5,2,48,48]{4,3,2,1,0:T(8,128)S(1)} %get-tuple-element.10) | data formatting | bytes 1474560 | tf_op jit(solution)/shard_map/reshape | solution.py:362
  51.1 2.6 %copy.11 = f32[1,1,8,5,4608]{4,2,3,1,0:T(8,128)} copy(f32[1,1,8,5,4608]{4,3,2,1,0:T(8,128)} %reshape.29) | data formatting | bytes 1474560 | tf_op jit(solution)/shard_map/reshape | solution.py:362
  53.7 0.0 copy-done
  53.7 9.5 %shard_map.53 = f32[8,96]{1,0:T(8,128)S(1)} custom-call(f32[8,5,48,96]{3,2,1,0:T(8,128)S(1)} %get-tuple-element.11.blocks, f32[8,96]{1,0:T(8,128)S(1)} %bitcast.17), custom_call_target="tpu_custom_call" | custom-call | tf_op jit(solution)/shard_map/pallas_call | solution.py:346
  63.2 0.6 copy.18
  (3 shorter events, 0.0 us)
Async XLA Ops:
  3.8 7.0 %copy-start.4 = (bf16[2,24,4,3,16,128]{5,1,0,3,2,4:T(8,128)(2,1)}, bf16[2,24,4,3,16,128]{5,1,0,3,2,4:T(8,128)(2,1)S(1)}, u32[]{:S(2)}) copy-start(bf16[2,24,4,3,16,128]{5,1,0,3,2,4:T(8,128)(2,1)S(1)} %copy.16) | copy-start | bytes 7077892
  3.8 6.9 %copy-start.5 = (bf16[2,4,3,3,4,4,128]{6,5,4,3,2,1,0:T(4,128)(2,1)S(1)}, bf16[2,4,3,3,4,4,128]{6,5,4,3,2,1,0:T(4,128)(2,1)}, u32[]{:S(2)}) copy-start(bf16[2,4,3,3,4,4,128]{6,5,4,3,2,1,0:T(4,128)(2,1)} %param.4) | copy-start | bytes 884740
  3.9 27.5 %collective-permute-start.1 = (bf16[4,576,128]{2,1,0:T(8,128)(2,1)S(1)}, bf16[4,576,128]{2,1,0:T(8,128)(2,1)S(1)}, u32[]{:S(2)}, u32[]{:S(2)}) collective-permute-start(bf16[4,576,128]{2,1,0:T(8,128)(2,1)S(1)} %slice.11), channel_id=1, source_target_pairs={{0,3},{1,0},{2,1},{3,2},{4,7},{5,4},{6,5},{7,6},{8,11},{9,8},{10,9... | collective-permute-start | bytes 1769480 | tf_op jit(solution)/shard_map/ppermute | solution.py:295
  9.1 22.4 %collective-permute-start = (bf16[4,576,128]{2,1,0:T(8,128)(2,1)S(1)}, bf16[4,576,128]{2,1,0:T(8,128)(2,1)S(1)}, u32[]{:S(2)}, u32[]{:S(2)}) collective-permute-start(bf16[4,576,128]{2,1,0:T(8,128)(2,1)S(1)} %bitcast.22), channel_id=1, source_target_pairs={{0,28},{4,0},{8,4},{12,8},{16,12},{20,16},{24,20},{28,24},{1,29},{... | collective-permute-start | bytes 1769480 | tf_op jit(solution)/shard_map/ppermute | solution.py:295
  15.8 1.3 %copy-start.2 = (bf16[1024,1024]{1,0:T(8,128)(2,1)}, bf16[1024,1024]{1,0:T(8,128)(2,1)S(1)}, u32[]{:S(2)}) copy-start(bf16[1024,1024]{1,0:T(8,128)(2,1)S(1)} %get-tuple-element.9.place) | copy-start | bytes 6291460
  17.2 12.9 %copy-start.1 = (bf16[8,2,576,128]{3,2,1,0:T(8,128)(2,1)}, bf16[8,2,576,128]{3,2,1,0:T(8,128)(2,1)S(1)}, u32[]{:S(2)}) copy-start(bf16[8,2,576,128]{3,2,1,0:T(8,128)(2,1)S(1)} %get-tuple-element.7.v_ref) | copy-start | bytes 7077892
  30.1 1.3 %copy-start.3 = (f32[8,2,240,96]{3,2,1,0:T(8,128)}, f32[8,2,240,96]{3,2,1,0:T(8,128)S(1)}, u32[]{:S(2)}) copy-start(f32[8,2,240,96]{3,2,1,0:T(8,128)S(1)} %shard_map.51.plane_sums) | copy-start | bytes 4423684
  48.8 4.9 %copy-start = (f32[1,1,8,96]{3,2,1,0:T(8,128)S(1)}, f32[1,1,8,96]{3,2,1,0:T(8,128)}, u32[]{:S(2)}) copy-start(f32[1,1,8,96]{3,2,1,0:T(8,128)} %param.5) | copy-start | bytes 9220

commit v3 on v2

--- a/solution.py
+++ b/solution.py
@@ -33,23 +33,23 @@
 
 
 def place_hops(direction, slot, shifted, u_ref, a, h, right):
-    links = []
-    for q in range(2):
-        links.append([[u_ref[a, h, pl.ds(((q * 4 + direction) * 3 + row) * 3 + col, 1), :]
-                       for col in range(3)] for row in range(3)])
+    sums = [[shifted[s][d][0] + shifted[s][d][1] for d in range(3)] for s in range(4)]
     for c in range(3):
+        links = []
+        for d in range(3):
+            lr, li = [
+                jnp.broadcast_to(u_ref[a, h, pl.ds(((q * 4 + direction) * 3 + c) * 3 + d, 1), :], (8, 128))
+                for q in range(2)
+            ]
+            links.append((lr, li - lr, lr + li))
         hops = []
         for s in range(4):
-            re = None
-            im = None
+            totals = None
             for d in range(3):
-                lr, li = links[0][c][d], links[1][c][d]
-                vr, vi = shifted[s][d]
-                term_r = lr * vr - li * vi
-                term_i = lr * vi + li * vr
-                re = term_r if re is None else re + term_r
-                im = term_i if im is None else im + term_i
-            hops.append((re, im))
+                factors = (sums[s][d], shifted[s][d][0], shifted[s][d][1])
+                terms = [link[None] * f.reshape(3, 8, 128) for link, f in zip(links[d], factors)]
+                totals = terms if totals is None else [x + y for x, y in zip(totals, terms)]
+            hops.append(((totals[0] - totals[2]).reshape(24, 128), (totals[0] + totals[1]).reshape(24, 128)))
         for s in range(4):
             chi = s // 2
             same = (-hops[s][0], -hops[s][1])
@@ -141,7 +141,7 @@
 
 
 def line_kernel(v_ref, u_ref, face_t, face_z, place, plane_sums, blocks, stored,
-                far_t, far_z, left0, left1, right0, right1):
+                far_t, far_z, flat, left0, left1, right0, right1):
     wide = jnp.concatenate([face_t[k] for k in range(4)], 1)
     found = jnp.dot(wide, place[0:512, :], preferred_element_type=jnp.float32)
     for a in range(8):
@@ -198,8 +198,13 @@
         kept = [whole, pick(line, 0, 1).T, pick(line, 1, 2).T, pick(plane, 0, 1).T, pick(plane, 1, 2).T]
         for i, block in enumerate(kept):
             blocks[a, i] = block
-            stored[a, i, 0] = block[:, :48]
-            stored[a, i, 1] = block[:, 48:]
+            flat[pl.ds(pl.multiple_of(a * 240 + i * 48, 8), 48), 0:96] = block
+
+    for i in range(5):
+        for g in range(6):
+            group = [flat[pl.ds(i * 48 + g * 8 + v, 8, stride=240), :] for v in range(8)]
+            stored[i, :, 384 * g:384 * g + 384] = jnp.concatenate([x[:, :48] for x in group], 1)
+            stored[i, :, 2304 + 384 * g:2688 + 384 * g] = jnp.concatenate([x[:, 48:96] for x in group], 1)
 
 
 def coarse_kernel(axes, blocks, phi_ref, out_ref, phi, ahead, back, got, send, recv):
@@ -301,7 +306,7 @@
     face_t = shifted_2(vectors[0:4], "ta", -1)
     face_z = shifted_2(vectors[0::4], "sa", -1)
     vmem = pl.BlockSpec(memory_space=pltpu.VMEM)
-    limit = pltpu.CompilerParams(vmem_limit_bytes=48 * 1024 * 1024)
+    limit = pltpu.CompilerParams(vmem_limit_bytes=24 * 1024 * 1024)
     spread_v, spread_u, place = pl.pallas_call(
         spread_kernel,
         out_shape=(
@@ -331,13 +336,14 @@
         line_kernel,
         out_shape=(
             jax.ShapeDtypeStruct((8, 5, 48, 96), jnp.float32),
-            jax.ShapeDtypeStruct((8, 5, 2, 48, 48), jnp.float32),
+            jax.ShapeDtypeStruct((5, 8, 4608), jnp.float32),
         ),
         in_specs=[vmem] * 6,
         out_specs=(vmem, vmem),
         scratch_shapes=[
             pltpu.VMEM((8, 576, 128), jnp.bfloat16),
             pltpu.VMEM((8, 2, 576, 128), jnp.bfloat16),
+            pltpu.VMEM((1920, 128), jnp.float32),
         ] + operands + [pltpu.VMEM((2, 192, 1536), jnp.bfloat16)] * 2,
         compiler_params=limit,
         cost_estimate=pl.CostEstimate(flops=8_000_000_000, bytes_accessed=6_000_000, transcendentals=0),
@@ -357,9 +363,9 @@
             pltpu.SemaphoreType.DMA((2, 4)),
         ],
         compiler_params=pltpu.CompilerParams(
-            collective_id=0, has_side_effects=True, vmem_limit_bytes=48 * 1024 * 1024),
+            collective_id=0, has_side_effects=True, vmem_limit_bytes=16 * 1024 * 1024),
     )(blocks, rows)
-    stored = stored.reshape(1, 1, 8, 5, 4608)
+    stored = stored.transpose(1, 0, 2).reshape(1, 1, 8, 5, 4608)
     return stored, out.reshape(1, 1, 8, 96)
 
 

time: 64 us -> 51.5 us (0.80)
  local copies, waits for them, and re-layouts: 11.5 us -> 3.97 us
  Pallas kernels: 44.8 us -> 39.9 us
    reshape x2 -> x0, local copies, waits for them, and re-layouts: 4.91 us -> none  [per_device(): stored = stored.reshape(1, 1, 8, 5, 4608)]
    pallas_call x1, Pallas kernels: 17.4 us -> 14.6 us  [per_device(): pl.pallas_call(line_kernel, out_shape=(jax.ShapeDtypeStruct((8, 5, 48, 96...]
    unnamed x13 -> x5, local copies, waits for them, and re-layouts: 3.22 us -> 0.61 us
    pallas_call x1, Pallas kernels: 5.04 us -> 3.38 us  [per_device(): pl.pallas_call(spread_kernel, out_shape=(jax.ShapeDtypeStruct((8, 2, 576,...]
  transfers between devices with their start and end apart: 2 -> 2, of which waited for: 0 -> 0; matrix products, arithmetic and copies ran while one was open for 0% -> 0% of each run, Pallas kernels for 28% -> 31%
where the time goes in v3:
time: 51.5 us; the launch traced here: 51.3 us
  Pallas kernels  39.9 us (77%)
  starting transfers between devices  6.76 us (13%)
  local copies, waits for them, and re-layouts  3.97 us (8%)
  between operations  0.69 us (1%)
    pallas_call x1, Pallas kernels, per_device(): pl.pallas_call(line_kernel, out_shape=(jax.ShapeDtypeStruct((8, 5, 48, 96...  14.6 us
    pallas_call x1, Pallas kernels, per_device(): pl.pallas_call(plane_kernel, out_shape=jax.ShapeDtypeStruct((8, 2, 240, 9...  12.5 us
    pallas_call x1, Pallas kernels, per_device(): pl.pallas_call(functools.partial(coarse_kernel, ('ta', 'sa')), out_shape=...  9.47 us
    ppermute x2, starting transfers between devices, shifted_2(): return lax.ppermute(value, axis, pairs)  6.76 us
    pallas_call x1, Pallas kernels, per_device(): pl.pallas_call(spread_kernel, out_shape=(jax.ShapeDtypeStruct((8, 2, 576,...  3.38 us
    reshape x1, local copies, waits for them, and re-layouts, per_device(): null_vectors.reshape(2, 24, 4, 3, 16, 128).transpose(4, 2, 3, 0, 1, 5)  3.19 us
  transfers between devices with their start and end apart: 2, of which 0 were waited for; matrix products, arithmetic and copies ran while one was open for 0% of the time, Pallas kernels for 31%

profile of v3, /device:TPU:0, one launch (start us, length us, event | category | flops | bytes accessed | tf_op | source)
XLA Modules:
  0.0 51.3 jit_solution(5196850015351136897)
XLA Ops:
  0.6 3.2 %copy.13 = bf16[2,24,4,3,16,128]{5,1,0,3,2,4:T(8,128)(2,1)S(1)} copy(bf16[2,24,4,3,16,128]{5,4,3,2,1,0:T(8,128)(2,1)} %bitcast.22) | data formatting | bytes 4718592 | tf_op jit(solution)/shard_map/reshape | solution.py:304
  3.8 0.0 copy-start.1
  3.9 5.1 %collective-permute-start.1 = (bf16[4,576,128]{2,1,0:T(8,128)(2,1)S(1)}, bf16[4,576,128]{2,1,0:T(8,128)(2,1)S(1)}, u32[]{:S(2)}, u32[]{:S(2)}) collective-permute-start(bf16[4,576,128]{2,1,0:T(8,128)(2,1)S(1)} %slice.11), channel_id=1, source_target_pairs={{0,3},{1,0},{2,1},{3,2},{4,7},{5,4},{6,5},{7,6},{8,11},{9,8},{10,9... | collective-permute-start | bytes 1769480 | tf_op jit(solution)/shard_map/ppermute | solution.py:300
  9.0 0.1 slice.12
  9.0 1.7 %collective-permute-start = (bf16[4,576,128]{2,1,0:T(8,128)(2,1)S(1)}, bf16[4,576,128]{2,1,0:T(8,128)(2,1)S(1)}, u32[]{:S(2)}, u32[]{:S(2)}) collective-permute-start(bf16[4,576,128]{2,1,0:T(8,128)(2,1)S(1)} %bitcast.23), channel_id=1, source_target_pairs={{0,28},{4,0},{8,4},{12,8},{16,12},{20,16},{24,20},{28,24},{1,29},{... | collective-permute-start | bytes 1769480 | tf_op jit(solution)/shard_map/ppermute | solution.py:300
  10.7 0.0 copy-done.1
  10.7 0.1 copy.12
  10.8 3.4 %shard_map.50 = (bf16[8,2,576,128]{3,2,1,0:T(8,128)(2,1)S(1)}, f32[8,2,72,128]{3,2,1,0:T(8,128)S(1)}, bf16[1024,1024]{1,0:T(8,128)(2,1)S(1)}) custom-call(bf16[16,576,128]{2,1,0:T(8,128)(2,1)S(1)} %bitcast.18, bf16[16,72,128]{2,1,0:T(8,128)(2,1)S(1)} %bitcast.19), custom_call_target="tpu_custom_call" | custom-call | flops 2700000000 | bytes 7000000 | tf_op jit(solution)/shard_map/pallas_call | solution.py:310
  14.2 12.5 %shard_map.51.plane_sums = f32[8,2,240,96]{3,2,1,0:T(8,128)S(1)} custom-call(bf16[8,2,576,128]{3,2,1,0:T(8,128)(2,1)S(1)} %get-tuple-element.7.v_ref, f32[8,2,72,128]{3,2,1,0:T(8,128)S(1)} %get-tuple-element.8.u_ref), custom_call_target="tpu_custom_call" | custom-call | flops 8000000000 | bytes 4000000 | tf_op jit(solution)/shard_map/pallas_call | solution.py:326
  26.6 0.0 collective-permute-done.1.face_z
  26.7 0.0 collective-permute-done.face_t
  26.7 0.0 copy-start
  26.7 14.6 %shard_map.52 = (f32[8,5,48,96]{3,2,1,0:T(8,128)S(1)}, f32[5,8,4608]{2,1,0:T(8,128)}) custom-call(bf16[8,2,576,128]{3,2,1,0:T(8,128)(2,1)S(1)} %get-tuple-element.7.v_ref, f32[8,2,72,128]{3,2,1,0:T(8,128)S(1)} %get-tuple-element.8.u_ref, bf16[4,576,128]{2,1,0:T(8,128)(2,1)S(1)} %collective-permute-done.face_t, ...), custom_call_target="tpu_custom_call" | custom-call | flops 8000000000 | bytes 6000000 | tf_op jit(solution)/shard_map/pallas_call | solution.py:335
  41.3 0.0 copy-done
  41.3 9.5 %shard_map.53 = f32[8,96]{1,0:T(8,128)S(1)} custom-call(f32[8,5,48,96]{3,2,1,0:T(8,128)S(1)} %get-tuple-element.11.blocks, f32[8,96]{1,0:T(8,128)S(1)} %bitcast.21), custom_call_target="tpu_custom_call" | custom-call | tf_op jit(solution)/shard_map/pallas_call | solution.py:352
  50.7 0.6 %copy.15 = f32[1,1,8,96]{3,2,1,0:T(8,128)} copy(f32[1,1,8,96]{3,2,1,0:T(8,128)S(1)} %bitcast.20) | data formatting | bytes 6144
  (1 shorter events, 0.0 us)
Async XLA Ops:
  3.8 6.9 %copy-start.1 = (bf16[2,4,3,3,4,4,128]{6,5,4,3,2,1,0:T(4,128)(2,1)S(1)}, bf16[2,4,3,3,4,4,128]{6,5,4,3,2,1,0:T(4,128)(2,1)}, u32[]{:S(2)}) copy-start(bf16[2,4,3,3,4,4,128]{6,5,4,3,2,1,0:T(4,128)(2,1)} %param.4) | copy-start | bytes 884740
  3.9 22.8 %collective-permute-start.1 = (bf16[4,576,128]{2,1,0:T(8,128)(2,1)S(1)}, bf16[4,576,128]{2,1,0:T(8,128)(2,1)S(1)}, u32[]{:S(2)}, u32[]{:S(2)}) collective-permute-start(bf16[4,576,128]{2,1,0:T(8,128)(2,1)S(1)} %slice.11), channel_id=1, source_target_pairs={{0,3},{1,0},{2,1},{3,2},{4,7},{5,4},{6,5},{7,6},{8,11},{9,8},{10,9... | collective-permute-start | bytes 1769480 | tf_op jit(solution)/shard_map/ppermute | solution.py:300
  9.0 17.6 %collective-permute-start = (bf16[4,576,128]{2,1,0:T(8,128)(2,1)S(1)}, bf16[4,576,128]{2,1,0:T(8,128)(2,1)S(1)}, u32[]{:S(2)}, u32[]{:S(2)}) collective-permute-start(bf16[4,576,128]{2,1,0:T(8,128)(2,1)S(1)} %bitcast.23), channel_id=1, source_target_pairs={{0,28},{4,0},{8,4},{12,8},{16,12},{20,16},{24,20},{28,24},{1,29},{... | collective-permute-start | bytes 1769480 | tf_op jit(solution)/shard_map/ppermute | solution.py:300
  26.7 14.6 %copy-start = (f32[1,1,8,96]{3,2,1,0:T(8,128)S(1)}, f32[1,1,8,96]{3,2,1,0:T(8,128)}, u32[]{:S(2)}) copy-start(f32[1,1,8,96]{3,2,1,0:T(8,128)} %param.5) | copy-start | bytes 9220

commit v4 on v3

--- a/solution.py
+++ b/solution.py
@@ -25,53 +25,71 @@
     return im, -re
 
 
-def hop_rows(same, cross, chi):
-    first, second = (same, cross) if chi == 0 else (cross, same)
-    of_real = jnp.concatenate([first[0], second[0], first[1], second[1]], 0)
-    of_imag = jnp.concatenate([first[1], second[1], -first[0], -second[0]], 0)
-    return of_real.astype(jnp.bfloat16), of_imag.astype(jnp.bfloat16)
-
-
-def place_hops(direction, slot, shifted, u_ref, a, h, right):
-    sums = [[shifted[s][d][0] + shifted[s][d][1] for d in range(3)] for s in range(4)]
+def place_hops(directions, shifted, u_ref, a, h, flip, right):
+    sums = [[[f[s][d][0] + f[s][d][1] for d in range(3)] for s in range(4)] for f in shifted]
     for c in range(3):
-        links = []
-        for d in range(3):
-            lr, li = [
-                jnp.broadcast_to(u_ref[a, h, pl.ds(((q * 4 + direction) * 3 + c) * 3 + d, 1), :], (8, 128))
-                for q in range(2)
-            ]
-            links.append((lr, li - lr, lr + li))
         hops = []
+        for slot, direction in enumerate(directions):
+            links = []
+            for d in range(3):
+                lr, li = [
+                    jnp.broadcast_to(u_ref[a, h, pl.ds(((q * 4 + direction) * 3 + c) * 3 + d, 1), :], (8, 128))
+                    for q in range(2)
+                ]
+                links.append((lr, li - lr, lr + li))
+            of_spin = []
+            for s in range(4):
+                totals = None
+                for d in range(3):
+                    factors = (sums[slot][s][d], shifted[slot][s][d][0], shifted[slot][s][d][1])
+                    terms = [link[None] * f.reshape(3, 8, 128) for link, f in zip(links[d], factors)]
+                    totals = terms if totals is None else [x + y for x, y in zip(totals, terms)]
+                of_spin.append(((totals[0] - totals[2]).reshape(24, 128), (totals[0] + totals[1]).reshape(24, 128)))
+            hops.append(of_spin)
         for s in range(4):
-            totals = None
-            for d in range(3):
-                factors = (sums[s][d], shifted[s][d][0], shifted[s][d][1])
-                terms = [link[None] * f.reshape(3, 8, 128) for link, f in zip(links[d], factors)]
-                totals = terms if totals is None else [x + y for x, y in zip(totals, terms)]
-            hops.append(((totals[0] - totals[2]).reshape(24, 128), (totals[0] + totals[1]).reshape(24, 128)))
-        for s in range(4):
-            chi = s // 2
-            same = (-hops[s][0], -hops[s][1])
-            power = PHASE[direction][chi]
-            if ODD_SIGN[direction] and s % 2 == 1:
-                power = (power + 2) % 4
-            cross = turn(*hops[SOURCE[direction][s]], power)
-            of_real, of_imag = hop_rows(same, cross, chi)
+            other = SOURCE[directions[0]][s]
             k = (s % 2) * 3 + c
-            right[chi, 96 * slot:96 * slot + 96, 128 * k:128 * k + 128] = of_real
-            right[chi, 96 * slot:96 * slot + 96, 128 * (k + 6):128 * (k + 7)] = of_imag
+            k_cross = (other % 2) * 3 + c
+            for q in range(2):
+                both = jnp.concatenate([hops[0][s][q], hops[1][s][q]], 0).astype(jnp.bfloat16)
+                right[s // 2, 48 * q:48 * q + 48, 128 * k:128 * k + 128] = both
+                if other % 2 == 1:
+                    both = both * flip
+                right[other // 2, 96 + 48 * q:144 + 48 * q, 128 * k_cross:128 * k_cross + 128] = both
 
 
 def place_left(values, edges, left):
     for s in range(4):
         for c in range(3):
-            for q in range(2):
-                part = values[s][c][q]
+            rows = []
+            for part in values[s][c]:
                 zero = jnp.zeros_like(part)
-                rows = [part, jnp.where(edges[0], part, zero), jnp.where(edges[1], part, zero), zero]
-                k = q * 6 + (s % 2) * 3 + c
-                left[s // 2, :, 128 * k:128 * k + 128] = jnp.concatenate(rows, 0).astype(jnp.bfloat16)
+                rows += [part, jnp.where(edges[0], part, zero), jnp.where(edges[1], part, zero)]
+            k = (s % 2) * 3 + c
+            left[s // 2, :, 128 * k:128 * k + 128] = jnp.concatenate(rows, 0).astype(jnp.bfloat16)
+
+
+def joined(of_re, of_im):
+    return of_re[:, :72] + of_im[:, 72:], of_im[:, :72] - of_re[:, 72:]
+
+
+def combine(raw, directions, chi):
+    same = joined(raw[0:48], raw[48:96])
+    cross = joined(raw[96:144], raw[144:192])
+    rows = []
+    for slot, direction in enumerate(directions):
+        span = slice(24 * slot, 24 * slot + 24)
+        pair = [(-same[0][span], -same[1][span]), turn(cross[0][span], cross[1][span], PHASE[direction][chi])]
+        first, second = pair if chi == 0 else pair[::-1]
+        rows += [first[0], second[0], first[1], second[1]]
+    if raw.shape[0] == 240:
+        rows += joined(raw[192:216], raw[216:240])
+    return jnp.concatenate(rows, 0)
+
+
+def flips(odd_slot):
+    row = lax.broadcasted_iota(jnp.int32, (48, 128), 0)
+    return jnp.where(row // 24 == odd_slot, -1.0, 1.0).astype(jnp.bfloat16)
 
 
 def load(ref, *index):
@@ -111,6 +129,7 @@
 
 def plane_kernel(v_ref, u_ref, sums, left0, left1, right0, right1):
     lane = lax.broadcasted_iota(jnp.int32, (24, 128), 1)
+    flip = flips(0)
     y_edge = lane // 4 % 4 == 3
     x_edge = lane % 4 == 3
 
@@ -132,12 +151,11 @@
                     k = (s % 2) * 3 + c
                     right[s // 2, 192:240, 128 * k:128 * k + 128] = (
                         jnp.concatenate([vr, vi], 0).astype(jnp.bfloat16))
-                    right[s // 2, 192:240, 128 * (k + 6):128 * (k + 7)] = (
-                        jnp.concatenate([vi, -vr], 0).astype(jnp.bfloat16))
-            place_hops(2, 0, moved(ahead_y, values), u_ref, a, h, right)
-            place_hops(3, 1, moved(ahead_x, values, load(v_ref, after, h)), u_ref, a, h, right)
+            ahead = (moved(ahead_y, values), moved(ahead_x, values, load(v_ref, after, h)))
+            place_hops((2, 3), ahead, u_ref, a, h, flip, right)
         for chi in range(2):
-            sums[a, chi] = product(right0[chi], left0[chi]) + product(right1[chi], left1[chi])
+            raw = product(right0[chi], left0[chi]) + product(right1[chi], left1[chi])
+            sums[a, chi] = combine(raw, (2, 3), chi)
 
 
 def line_kernel(v_ref, u_ref, face_t, face_z, place, plane_sums, blocks, stored,
@@ -154,6 +172,7 @@
             far_z[a, h] = found[:, 128 * a:128 * a + 128].astype(jnp.bfloat16)
 
     lane = lax.broadcasted_iota(jnp.int32, (24, 128), 1)
+    flip = flips(1)
     upper = lane >= 64
     z_edge = lane // 16 % 4 == 3
     nowhere = lane < 0
@@ -174,12 +193,13 @@
             values = load(v_ref, a, h)
             place_left(values, (upper if h == 1 else nowhere, z_edge), left)
             following = load(v_ref, a, 1) if h == 0 else load(far_t, a)
-            place_hops(0, 0, moved(ahead_t, values, following), u_ref, a, h, right)
-            place_hops(1, 1, moved(ahead_z, values, load(far_z, a, h)), u_ref, a, h, right)
+            ahead = (moved(ahead_t, values, following), moved(ahead_z, values, load(far_z, a, h)))
+            place_hops((0, 1), ahead, u_ref, a, h, flip, right)
         line = []
         plane = []
         for chi in range(2):
-            line.append(product(right0[chi], left0[chi]) + product(right1[chi], left1[chi]))
+            raw = product(right0[chi], left0[chi]) + product(right1[chi], left1[chi])
+            line.append(combine(raw, (0, 1), chi))
             plane.append(plane_sums[a, chi])
 
         def pick(sums, slot, kind):
@@ -320,15 +340,15 @@
         cost_estimate=pl.CostEstimate(flops=2_700_000_000, bytes_accessed=7_000_000, transcendentals=0),
     )(vectors, links)
     operands = [
-        pltpu.VMEM((2, 96, 1536), jnp.bfloat16),
-        pltpu.VMEM((2, 96, 1536), jnp.bfloat16),
+        pltpu.VMEM((2, 144, 768), jnp.bfloat16),
+        pltpu.VMEM((2, 144, 768), jnp.bfloat16),
     ]
     plane_sums = pl.pallas_call(
         plane_kernel,
-        out_shape=jax.ShapeDtypeStruct((8, 2, 240, 96), jnp.float32),
+        out_shape=jax.ShapeDtypeStruct((8, 2, 240, 72), jnp.float32),
         in_specs=[vmem] * 2,
         out_specs=vmem,
-        scratch_shapes=operands + [pltpu.VMEM((2, 240, 1536), jnp.bfloat16)] * 2,
+        scratch_shapes=operands + [pltpu.VMEM((2, 240, 768), jnp.bfloat16)] * 2,
         compiler_params=limit,
         cost_estimate=pl.CostEstimate(flops=8_000_000_000, bytes_accessed=4_000_000, transcendentals=0),
     )(spread_v, spread_u)
@@ -344,7 +364,7 @@
             pltpu.VMEM((8, 576, 128), jnp.bfloat16),
             pltpu.VMEM((8, 2, 576, 128), jnp.bfloat16),
             pltpu.VMEM((1920, 128), jnp.float32),
-        ] + operands + [pltpu.VMEM((2, 192, 1536), jnp.bfloat16)] * 2,
+        ] + operands + [pltpu.VMEM((2, 192, 768), jnp.bfloat16)] * 2,
         compiler_params=limit,
         cost_estimate=pl.CostEstimate(flops=8_000_000_000, bytes_accessed=6_000_000, transcendentals=0),
     )(spread_v, spread_u, face_t, face_z, place, plane_sums)

time: 51.5 us -> 48.6 us (0.944)
  Pallas kernels: 39.9 us -> 37 us
    pallas_call x1, Pallas kernels: 12.5 us -> 10.2 us  [per_device(): pl.pallas_call(plane_kernel, out_shape=jax.ShapeDtypeStruct((8, 2, 240, 7...]
    pallas_call x1, Pallas kernels: 14.6 us -> 13.5 us  [per_device(): pl.pallas_call(line_kernel, out_shape=(jax.ShapeDtypeStruct((8, 5, 48, 96...]
  transfers between devices with their start and end apart: 2 -> 2, of which waited for: 0 -> 0; matrix products, arithmetic and copies ran while one was open for 0% -> 0% of each run, Pallas kernels for 31% -> 28%
where the time goes in v4:
time: 48.6 us; the launch traced here: 48.5 us
  Pallas kernels  37 us (76%)
  starting transfers between devices  6.76 us (14%)
  local copies, waits for them, and re-layouts  3.97 us (8%)
  between operations  0.7 us (1%)
    pallas_call x1, Pallas kernels, per_device(): pl.pallas_call(line_kernel, out_shape=(jax.ShapeDtypeStruct((8, 5, 48, 96...  13.5 us
    pallas_call x1, Pallas kernels, per_device(): pl.pallas_call(plane_kernel, out_shape=jax.ShapeDtypeStruct((8, 2, 240, 7...  10.2 us
    pallas_call x1, Pallas kernels, per_device(): pl.pallas_call(functools.partial(coarse_kernel, ('ta', 'sa')), out_shape=...  9.97 us
    ppermute x2, starting transfers between devices, shifted_2(): return lax.ppermute(value, axis, pairs)  6.76 us
    pallas_call x1, Pallas kernels, per_device(): pl.pallas_call(spread_kernel, out_shape=(jax.ShapeDtypeStruct((8, 2, 576,...  3.38 us
    reshape x1, local copies, waits for them, and re-layouts, per_device(): null_vectors.reshape(2, 24, 4, 3, 16, 128).transpose(4, 2, 3, 0, 1, 5)  3.19 us
  transfers between devices with their start and end apart: 2, of which 0 were waited for; matrix products, arithmetic and copies ran while one was open for 0% of the time, Pallas kernels for 28%

profile of v4, /device:TPU:0, one launch (start us, length us, event | category | flops | bytes accessed | tf_op | source)
XLA Modules:
  0.0 48.5 jit_solution(823175392864690166)
XLA Ops:
  0.6 3.2 %copy.13 = bf16[2,24,4,3,16,128]{5,1,0,3,2,4:T(8,128)(2,1)S(1)} copy(bf16[2,24,4,3,16,128]{5,4,3,2,1,0:T(8,128)(2,1)} %bitcast.22) | data formatting | bytes 4718592 | tf_op jit(solution)/shard_map/reshape | solution.py:324
  3.8 0.0 copy-start.1
  3.9 5.1 %collective-permute-start.1 = (bf16[4,576,128]{2,1,0:T(8,128)(2,1)S(1)}, bf16[4,576,128]{2,1,0:T(8,128)(2,1)S(1)}, u32[]{:S(2)}, u32[]{:S(2)}) collective-permute-start(bf16[4,576,128]{2,1,0:T(8,128)(2,1)S(1)} %slice.11), channel_id=1, source_target_pairs={{0,3},{1,0},{2,1},{3,2},{4,7},{5,4},{6,5},{7,6},{8,11},{9,8},{10,9... | collective-permute-start | bytes 1769480 | tf_op jit(solution)/shard_map/ppermute | solution.py:320
  9.0 0.1 slice.12
  9.0 1.7 %collective-permute-start = (bf16[4,576,128]{2,1,0:T(8,128)(2,1)S(1)}, bf16[4,576,128]{2,1,0:T(8,128)(2,1)S(1)}, u32[]{:S(2)}, u32[]{:S(2)}) collective-permute-start(bf16[4,576,128]{2,1,0:T(8,128)(2,1)S(1)} %bitcast.23), channel_id=1, source_target_pairs={{0,28},{4,0},{8,4},{12,8},{16,12},{20,16},{24,20},{28,24},{1,29},{... | collective-permute-start | bytes 1769480 | tf_op jit(solution)/shard_map/ppermute | solution.py:320
  10.7 0.0 copy-done.1
  10.7 0.1 copy.12
  10.8 3.4 %shard_map.50 = (bf16[8,2,576,128]{3,2,1,0:T(8,128)(2,1)S(1)}, f32[8,2,72,128]{3,2,1,0:T(8,128)S(1)}, bf16[1024,1024]{1,0:T(8,128)(2,1)S(1)}) custom-call(bf16[16,576,128]{2,1,0:T(8,128)(2,1)S(1)} %bitcast.18, bf16[16,72,128]{2,1,0:T(8,128)(2,1)S(1)} %bitcast.19), custom_call_target="tpu_custom_call" | custom-call | flops 2700000000 | bytes 7000000 | tf_op jit(solution)/shard_map/pallas_call | solution.py:330
  14.2 10.2 %shard_map.51.plane_sums = f32[8,2,240,72]{3,2,1,0:T(8,128)S(1)} custom-call(bf16[8,2,576,128]{3,2,1,0:T(8,128)(2,1)S(1)} %get-tuple-element.7.v_ref, f32[8,2,72,128]{3,2,1,0:T(8,128)S(1)} %get-tuple-element.8.u_ref), custom_call_target="tpu_custom_call" | custom-call | flops 8000000000 | bytes 4000000 | tf_op jit(solution)/shard_map/pallas_call | solution.py:346
  24.4 0.0 collective-permute-done.1.face_z
  24.4 0.0 collective-permute-done.face_t
  24.4 0.0 copy-start
  24.4 13.5 %shard_map.52 = (f32[8,5,48,96]{3,2,1,0:T(8,128)S(1)}, f32[5,8,4608]{2,1,0:T(8,128)}) custom-call(bf16[8,2,576,128]{3,2,1,0:T(8,128)(2,1)S(1)} %get-tuple-element.7.v_ref, f32[8,2,72,128]{3,2,1,0:T(8,128)S(1)} %get-tuple-element.8.u_ref, bf16[4,576,128]{2,1,0:T(8,128)(2,1)S(1)} %collective-permute-done.face_t, ...), custom_call_target="tpu_custom_call" | custom-call | flops 8000000000 | bytes 6000000 | tf_op jit(solution)/shard_map/pallas_call | solution.py:355
  37.9 0.0 copy-done
  37.9 10.0 %shard_map.53 = f32[8,96]{1,0:T(8,128)S(1)} custom-call(f32[8,5,48,96]{3,2,1,0:T(8,128)S(1)} %get-tuple-element.11.blocks, f32[8,96]{1,0:T(8,128)S(1)} %bitcast.21), custom_call_target="tpu_custom_call" | custom-call | tf_op jit(solution)/shard_map/pallas_call | solution.py:372
  47.9 0.6 %copy.15 = f32[1,1,8,96]{3,2,1,0:T(8,128)} copy(f32[1,1,8,96]{3,2,1,0:T(8,128)S(1)} %bitcast.20) | data formatting | bytes 6144
  (1 shorter events, 0.0 us)
Async XLA Ops:
  3.8 6.9 %copy-start.1 = (bf16[2,4,3,3,4,4,128]{6,5,4,3,2,1,0:T(4,128)(2,1)S(1)}, bf16[2,4,3,3,4,4,128]{6,5,4,3,2,1,0:T(4,128)(2,1)}, u32[]{:S(2)}) copy-start(bf16[2,4,3,3,4,4,128]{6,5,4,3,2,1,0:T(4,128)(2,1)} %param.4) | copy-start | bytes 884740
  3.9 20.5 %collective-permute-start.1 = (bf16[4,576,128]{2,1,0:T(8,128)(2,1)S(1)}, bf16[4,576,128]{2,1,0:T(8,128)(2,1)S(1)}, u32[]{:S(2)}, u32[]{:S(2)}) collective-permute-start(bf16[4,576,128]{2,1,0:T(8,128)(2,1)S(1)} %slice.11), channel_id=1, source_target_pairs={{0,3},{1,0},{2,1},{3,2},{4,7},{5,4},{6,5},{7,6},{8,11},{9,8},{10,9... | collective-permute-start | bytes 1769480 | tf_op jit(solution)/shard_map/ppermute | solution.py:320
  9.0 15.3 %collective-permute-start = (bf16[4,576,128]{2,1,0:T(8,128)(2,1)S(1)}, bf16[4,576,128]{2,1,0:T(8,128)(2,1)S(1)}, u32[]{:S(2)}, u32[]{:S(2)}) collective-permute-start(bf16[4,576,128]{2,1,0:T(8,128)(2,1)S(1)} %bitcast.23), channel_id=1, source_target_pairs={{0,28},{4,0},{8,4},{12,8},{16,12},{20,16},{24,20},{28,24},{1,29},{... | collective-permute-start | bytes 1769480 | tf_op jit(solution)/shard_map/ppermute | solution.py:320
  24.4 13.5 %copy-start = (f32[1,1,8,96]{3,2,1,0:T(8,128)S(1)}, f32[1,1,8,96]{3,2,1,0:T(8,128)}, u32[]{:S(2)}) copy-start(f32[1,1,8,96]{3,2,1,0:T(8,128)} %param.5) | copy-start | bytes 9220

commit v5 on v4

--- a/solution.py
+++ b/solution.py
@@ -11,7 +11,6 @@
 MESH = pl.DeviceIdType.MESH
 
 SOURCE = ((2, 3, 0, 1), (2, 3, 0, 1), (3, 2, 1, 0), (3, 2, 1, 0))
-ODD_SIGN = (False, True, True, False)
 PHASE = ((0, 0), (3, 1), (2, 0), (3, 1))
 
 
@@ -142,6 +141,7 @@
     @pl.loop(0, 8)
     def _(a):
         after = lax.rem(a + 1, 8)
+        halves = []
         for h, (left, right) in enumerate(((left0, right0), (left1, right1))):
             values = load(v_ref, a, h)
             place_left(values, (y_edge, x_edge), left)
@@ -153,8 +153,9 @@
                         jnp.concatenate([vr, vi], 0).astype(jnp.bfloat16))
             ahead = (moved(ahead_y, values), moved(ahead_x, values, load(v_ref, after, h)))
             place_hops((2, 3), ahead, u_ref, a, h, flip, right)
+            halves.append([product(right[chi], left[chi]) for chi in range(2)])
         for chi in range(2):
-            raw = product(right0[chi], left0[chi]) + product(right1[chi], left1[chi])
+            raw = halves[0][chi] + halves[1][chi]
             sums[a, chi] = combine(raw, (2, 3), chi)
 
 
@@ -189,16 +190,18 @@
 
     @pl.loop(0, 8)
     def _(a):
+        halves = []
         for h, (left, right) in enumerate(((left0, right0), (left1, right1))):
             values = load(v_ref, a, h)
             place_left(values, (upper if h == 1 else nowhere, z_edge), left)
             following = load(v_ref, a, 1) if h == 0 else load(far_t, a)
             ahead = (moved(ahead_t, values, following), moved(ahead_z, values, load(far_z, a, h)))
             place_hops((0, 1), ahead, u_ref, a, h, flip, right)
+            halves.append([product(right[chi], left[chi]) for chi in range(2)])
         line = []
         plane = []
         for chi in range(2):
-            raw = product(right0[chi], left0[chi]) + product(right1[chi], left1[chi])
+            raw = halves[0][chi] + halves[1][chi]
             line.append(combine(raw, (0, 1), chi))
             plane.append(plane_sums[a, chi])
 
@@ -323,8 +326,6 @@
 def per_device(null_vectors, gauge_links, coarse_in):
     vectors = null_vectors.reshape(2, 24, 4, 3, 16, 128).transpose(4, 2, 3, 0, 1, 5).reshape(16, 576, 128)
     links = gauge_links.reshape(72, 16, 128).transpose(1, 0, 2)
-    face_t = shifted_2(vectors[0:4], "ta", -1)
-    face_z = shifted_2(vectors[0::4], "sa", -1)
     vmem = pl.BlockSpec(memory_space=pltpu.VMEM)
     limit = pltpu.CompilerParams(vmem_limit_bytes=24 * 1024 * 1024)
     spread_v, spread_u, place = pl.pallas_call(
@@ -339,6 +340,9 @@
         compiler_params=limit,
         cost_estimate=pl.CostEstimate(flops=2_700_000_000, bytes_accessed=7_000_000, transcendentals=0),
     )(vectors, links)
+    vectors, spread_v = lax.optimization_barrier((vectors, spread_v))
+    face_t = shifted_2(vectors[0:4], "ta", -1)
+    face_z = shifted_2(vectors[0::4], "sa", -1)
     operands = [
         pltpu.VMEM((2, 144, 768), jnp.bfloat16),
         pltpu.VMEM((2, 144, 768), jnp.bfloat16),

time: 48.6 us -> 53.2 us (1.095)
  Pallas kernels: 37 us -> 40 us
  local copies, waits for them, and re-layouts: 3.97 us -> 4.92 us
  waiting for transfers between devices: 0.01 us -> 0.71 us
    pallas_call x1, Pallas kernels: 9.97 us -> 12.8 us  [per_device(): pl.pallas_call(functools.partial(coarse_kernel, ('ta', 'sa')), out_shape=...]
    reshape x1, local copies, waits for them, and re-layouts: 0.08 us -> 1.04 us  [per_device(): links = gauge_links.reshape(72, 16, 128).transpose(1, 0, 2)]
    ppermute x2, waiting for transfers between devices: 0.01 us -> 0.71 us  [shifted_2(): return lax.ppermute(value, axis, pairs)]
  transfers between devices with their start and end apart: 2 -> 2, of which waited for: 0 -> 1; matrix products, arithmetic and copies ran while one was open for 0% -> 0% of each run, Pallas kernels for 28% -> 19%
where the time goes in v5:
time: 53.2 us; the launch traced here: 53 us
  Pallas kernels  40 us (75%)
  starting transfers between devices  6.71 us (13%)
  local copies, waits for them, and re-layouts  4.92 us (9%)
  waiting for transfers between devices  0.71 us (1%)
  between operations  0.66 us (1%)
    pallas_call x1, Pallas kernels, per_device(): pl.pallas_call(line_kernel, out_shape=(jax.ShapeDtypeStruct((8, 5, 48, 96...  13.6 us
    pallas_call x1, Pallas kernels, per_device(): pl.pallas_call(functools.partial(coarse_kernel, ('ta', 'sa')), out_shape=...  12.8 us
    pallas_call x1, Pallas kernels, per_device(): pl.pallas_call(plane_kernel, out_shape=jax.ShapeDtypeStruct((8, 2, 240, 7...  10.3 us
    ppermute x2, starting transfers between devices, shifted_2(): return lax.ppermute(value, axis, pairs)  6.71 us
    pallas_call x1, Pallas kernels, per_device(): pl.pallas_call(spread_kernel, out_shape=(jax.ShapeDtypeStruct((8, 2, 576,...  3.42 us
    reshape x1, local copies, waits for them, and re-layouts, per_device(): null_vectors.reshape(2, 24, 4, 3, 16, 128).transpose(4, 2, 3, 0, 1, 5)  3.19 us
  transfers between devices with their start and end apart: 2, of which 1 were waited for; matrix products, arithmetic and copies ran while one was open for 0% of the time, Pallas kernels for 19%

profile of v5, /device:TPU:0, one launch (start us, length us, event | category | flops | bytes accessed | tf_op | source)
XLA Modules:
  0.0 53.0 jit_solution(5607429747592311319)
XLA Ops:
  0.6 1.0 %copy.10 = bf16[72,16,128]{2,0,1:T(8,128)(2,1)S(1)} copy(bf16[72,16,128]{2,1,0:T(8,128)(2,1)} %bitcast.19) | data formatting | bytes 589824 | tf_op jit(solution)/shard_map/reshape | solution.py:328
  1.7 3.2 %copy.7 = bf16[2,24,4,3,16,128]{5,1,0,3,2,4:T(8,128)(2,1)S(1)} copy(bf16[2,24,4,3,16,128]{5,4,3,2,1,0:T(8,128)(2,1)} %bitcast.18) | data formatting | bytes 4718592 | tf_op jit(solution)/shard_map/reshape | solution.py:327
  4.9 3.4 %shard_map.50 = (bf16[8,2,576,128]{3,2,1,0:T(8,128)(2,1)S(1)}, f32[8,2,72,128]{3,2,1,0:T(8,128)S(1)}, bf16[1024,1024]{1,0:T(8,128)(2,1)S(1)}) custom-call(bf16[16,576,128]{2,1,0:T(8,128)(2,1)S(1)} %bitcast.13, bf16[16,72,128]{2,1,0:T(8,128)(2,1)S(1)} %bitcast.15), custom_call_target="tpu_custom_call" | custom-call | flops 2700000000 | bytes 7000000 | tf_op jit(solution)/shard_map/pallas_call | solution.py:331
  8.3 0.1 fusion
  8.4 5.1 %collective-permute-start.1 = (bf16[4,576,128]{2,1,0:T(8,128)(2,1)S(1)}, bf16[4,576,128]{2,1,0:T(8,128)(2,1)S(1)}, u32[]{:S(2)}, u32[]{:S(2)}) collective-permute-start(bf16[4,576,128]{2,1,0:T(8,128)(2,1)S(1)} %get-tuple-element.16), channel_id=1, source_target_pairs={{0,3},{1,0},{2,1},{3,2},{4,7},{5,4},{6,5},{7,6},{8,11},{9,8},{10,9... | collective-permute-start | bytes 1769480 | tf_op jit(solution)/shard_map/ppermute | solution.py:323
  13.5 1.6 %collective-permute-start = (bf16[4,576,128]{2,1,0:T(8,128)(2,1)S(1)}, bf16[4,576,128]{2,1,0:T(8,128)(2,1)S(1)}, u32[]{:S(2)}, u32[]{:S(2)}) collective-permute-start(bf16[4,576,128]{2,1,0:T(8,128)(2,1)S(1)} %get-tuple-element.17), channel_id=1, source_target_pairs={{0,28},{4,0},{8,4},{12,8},{16,12},{20,16},{24,20},{28,24},{1,29},{... | collective-permute-start | bytes 1769480 | tf_op jit(solution)/shard_map/ppermute | solution.py:323
  15.1 10.3 %shard_map.51.plane_sums = f32[8,2,240,72]{3,2,1,0:T(8,128)S(1)} custom-call(bf16[8,2,576,128]{3,2,1,0:T(8,128)(2,1)S(1)} %get-tuple-element.10.v_ref, f32[8,2,72,128]{3,2,1,0:T(8,128)S(1)} %get-tuple-element.11.u_ref), custom_call_target="tpu_custom_call" | custom-call | flops 8000000000 | bytes 4000000 | tf_op jit(solution)/shard_map/pallas_call | solution.py:350
  25.4 0.7 %collective-permute-done.1.face_z = bf16[4,576,128]{2,1,0:T(8,128)(2,1)S(1)} collective-permute-done((bf16[4,576,128]{2,1,0:T(8,128)(2,1)S(1)}, bf16[4,576,128]{2,1,0:T(8,128)(2,1)S(1)}, u32[]{:S(2)}, u32[]{:S(2)}) %collective-permute-start.1) | collective-permute-done | bytes 589856 | tf_op jit(solution)/shard_map/ppermute | solution.py:323
  26.1 0.0 collective-permute-done.face_t
  26.1 0.0 copy-start
  26.1 13.6 %shard_map.52 = (f32[8,5,48,96]{3,2,1,0:T(8,128)S(1)}, f32[5,8,4608]{2,1,0:T(8,128)}) custom-call(bf16[8,2,576,128]{3,2,1,0:T(8,128)(2,1)S(1)} %get-tuple-element.10.v_ref, f32[8,2,72,128]{3,2,1,0:T(8,128)S(1)} %get-tuple-element.11.u_ref, bf16[4,576,128]{2,1,0:T(8,128)(2,1)S(1)} %collective-permute-done.face_t, ...), custom_call_target="tpu_custom_call" | custom-call | flops 8000000000 | bytes 6000000 | tf_op jit(solution)/shard_map/pallas_call | solution.py:359
  39.6 0.0 copy-done
  39.6 12.8 %shard_map.53 = f32[8,96]{1,0:T(8,128)S(1)} custom-call(f32[8,5,48,96]{3,2,1,0:T(8,128)S(1)} %get-tuple-element.15.blocks, f32[8,96]{1,0:T(8,128)S(1)} %bitcast.17), custom_call_target="tpu_custom_call" | custom-call | tf_op jit(solution)/shard_map/pallas_call | solution.py:376
  52.4 0.6 %copy.12 = f32[1,1,8,96]{3,2,1,0:T(8,128)} copy(f32[1,1,8,96]{3,2,1,0:T(8,128)S(1)} %bitcast.16) | data formatting | bytes 6144
Async XLA Ops:
  8.4 17.7 %collective-permute-start.1 = (bf16[4,576,128]{2,1,0:T(8,128)(2,1)S(1)}, bf16[4,576,128]{2,1,0:T(8,128)(2,1)S(1)}, u32[]{:S(2)}, u32[]{:S(2)}) collective-permute-start(bf16[4,576,128]{2,1,0:T(8,128)(2,1)S(1)} %get-tuple-element.16), channel_id=1, source_target_pairs={{0,3},{1,0},{2,1},{3,2},{4,7},{5,4},{6,5},{7,6},{8,11},{9,8},{10,9... | collective-permute-start | bytes 1769480 | tf_op jit(solution)/shard_map/ppermute | solution.py:323
  13.5 12.6 %collective-permute-start = (bf16[4,576,128]{2,1,0:T(8,128)(2,1)S(1)}, bf16[4,576,128]{2,1,0:T(8,128)(2,1)S(1)}, u32[]{:S(2)}, u32[]{:S(2)}) collective-permute-start(bf16[4,576,128]{2,1,0:T(8,128)(2,1)S(1)} %get-tuple-element.17), channel_id=1, source_target_pairs={{0,28},{4,0},{8,4},{12,8},{16,12},{20,16},{24,20},{28,24},{1,29},{... | collective-permute-start | bytes 1769480 | tf_op jit(solution)/shard_map/ppermute | solution.py:323
  26.1 13.6 %copy-start = (f32[1,1,8,96]{3,2,1,0:T(8,128)S(1)}, f32[1,1,8,96]{3,2,1,0:T(8,128)}, u32[]{:S(2)}) copy-start(f32[1,1,8,96]{3,2,1,0:T(8,128)} %param.5) | copy-start | bytes 9220
